TPU v7x, 32 devices: a whole 2x2x4 slice. The times are simulated.
32 devices in a mesh: section: 2 (over x), dp: 4 (over y, core), expert: 4 (over z).
Axes of the slice: x: 2, y: 2, z: 4, core: 2. Of those that a mesh axis runs over, the one named last changes fastest.
Arguments:
- patches: bfloat16 [8192, 1152], P(('dp', 'expert')), may hold values from -50 to 50
- lengths: int32 [16, 4], P(('dp', 'expert')), may hold values from 1 to 64, 128 in all within a row
- w_qkv: bfloat16 [1152, 3456], P(None, 'section'), may hold values from -4.714045 to 4.714045
- w_out: bfloat16 [1152, 1152], P('section'), may hold values from -0.1875 to 0.1875
- w_proj: bfloat16 [4608, 2048], P('dp', 'section'), may hold values from -0.09375 to 0.09375
- routes: int32 [2048, 6], P(('dp', 'expert')), may hold values from 0 to 15, all different within a row; in each aligned block of 128 rows (0 to 127, 128 to 255, ...) at most 96 rows name the same one
- gates: float32 [2048, 6], P(('dp', 'expert')), may hold values from 0.05 to 0.4
- w_gate: bfloat16 [16, 2048, 1408], P(('dp', 'expert'), None, 'section'), may hold values from -0.125 to 0.125
- w_up: bfloat16 [16, 2048, 1408], P(('dp', 'expert'), None, 'section'), may hold values from -0.125 to 0.125
- w_down: bfloat16 [16, 1408, 2048], P(('dp', 'expert'), 'section'), may hold values from -0.15625 to 0.15625
Outputs:
- language_out: bfloat16 [2048, 2048], P(('dp', 'expert'), 'section')
Inputs may be any that keep to these rules, and one draw needn't show every extreme that they name: Each row lists, in order, the lengths in merged tokens of a group's images; they sum to 128 and the largest is exactly 64. `routes`: A token's 6 experts differ. Among the rows of one device no expert is named more than 96 times, a bound that some block reaches in every draw.
All inputs are finite; a program needn't handle non-finite values.
Results may differ from a plain program's by a relative error of at most 0.012.
Values may be sent and summed in bfloat16 or wider, within the bound.
A program may use at most 64 MiB of HBM per device.

v0:
```python
import math

import jax
import jax.numpy as jnp
from jax import lax
from jax.sharding import PartitionSpec as P

D_VIT = 1152
HEADS = 16
TOP = 6


def layer_norm(values):
    center = values - jnp.mean(values, axis=-1, keepdims=True)
    spread = jnp.mean(center * center, axis=-1, keepdims=True)
    return center * lax.rsqrt(spread + 1e-06)


def rms_norm(values):
    return values * lax.rsqrt(jnp.mean(values * values, axis=-1, keepdims=True) + 1e-06)


def per_device(patches, lengths, w_qkv, w_out, w_proj, routes, gates, w_gate, w_up, w_down):
    data_count = lax.axis_size("dp")
    owner_count = lax.axis_size("expert")
    patch_rows, width = patches.shape
    head_dim = D_VIT // HEADS
    local_heads = w_qkv.shape[1] // (3 * head_dim)
    scale = 1.0 / math.sqrt(head_dim)
    normed_in = layer_norm(patches.astype(jnp.float32)).astype(jnp.bfloat16)
    packed = jnp.dot(normed_in, w_qkv, preferred_element_type=jnp.float32).astype(jnp.bfloat16)
    packed = packed.reshape(patch_rows, local_heads, 3, head_dim)
    query = packed[:, :, 0]
    key_part = packed[:, :, 1]
    value_part = packed[:, :, 2]
    ends = jnp.cumsum(lengths[0]) * 4
    places = jnp.arange(patch_rows, dtype=jnp.int32)
    segment = jnp.sum((places[:, None] >= ends[None, :]).astype(jnp.int32), axis=1)
    block_rows = min(patch_rows, 512)
    block_count = patch_rows // block_rows

    def attend(blocks):
        query_block, segment_block = blocks
        scores = (
            jnp.einsum("qhd,khd->hqk", query_block, key_part, preferred_element_type=jnp.float32)
            * scale
        )
        same = segment_block[:, None] == segment[None, :]
        scores = jnp.where(same[None], scores, -jnp.inf)
        peak = jnp.max(scores, axis=-1, keepdims=True)
        weights = jnp.where(same[None], jnp.exp(scores - peak), 0.0)
        probs = (weights / jnp.sum(weights, axis=-1, keepdims=True)).astype(jnp.bfloat16)
        result = jnp.einsum("hqk,khd->qhd", probs, value_part, preferred_element_type=jnp.float32)
        return result.astype(jnp.bfloat16).reshape(block_rows, local_heads * head_dim)

    attended = lax.map(
        attend,
        (
            query.reshape(block_count, block_rows, local_heads, head_dim),
            segment.reshape(block_count, block_rows),
        ),
    )
    attended = attended.reshape(patch_rows, local_heads * head_dim)
    merged_count = patch_rows // 4
    summed = lax.psum(
        jnp.dot(attended, w_out, preferred_element_type=jnp.float32).astype(jnp.bfloat16), "section"
    ).astype(jnp.float32)
    merged = (
        (patches.astype(jnp.float32) + summed).reshape(merged_count, 4 * width).astype(jnp.bfloat16)
    )
    proj_own = jnp.dot(
        merged, lax.all_gather(w_proj, "dp", axis=0, tiled=True), preferred_element_type=jnp.float32
    ).astype(jnp.bfloat16)
    projected = lax.all_gather(proj_own, "section", axis=1, tiled=True)
    model_width = projected.shape[1]
    normed_tokens = rms_norm(projected.astype(jnp.float32)).astype(jnp.bfloat16)
    expert_total = data_count * owner_count
    capacity = max(2, min(merged_count, 2 * merged_count * TOP // expert_total))
    route_flat = routes.reshape(-1)
    onehot = (route_flat[:, None] == jnp.arange(expert_total, dtype=jnp.int32)[None, :]).astype(
        jnp.int32
    )
    ranks = jnp.cumsum(onehot, axis=0) - 1
    slots = jnp.sum(ranks * onehot, axis=1)
    target = route_flat * capacity + slots
    owners = jnp.arange(merged_count * TOP, dtype=jnp.int32) // TOP
    source = jnp.zeros((expert_total * capacity,), dtype=jnp.int32).at[target].set(owners)
    outgoing = normed_tokens[source].reshape(expert_total, capacity, model_width)
    received = lax.all_to_all(outgoing, ("dp", "expert"), split_axis=0, concat_axis=0, tiled=True)
    flat_rows = received.reshape(-1, received.shape[-1])
    gate_act = jnp.dot(flat_rows, w_gate[0], preferred_element_type=jnp.float32)
    up_act = jnp.dot(flat_rows, w_up[0], preferred_element_type=jnp.float32)
    hidden = (jax.nn.silu(gate_act) * up_act).astype(jnp.bfloat16)
    result = jnp.dot(hidden, w_down[0], preferred_element_type=jnp.float32).astype(jnp.bfloat16)
    returned = lax.all_to_all(
        result.reshape(received.shape[:-1] + (w_down.shape[2],)),
        ("dp", "expert"),
        split_axis=0,
        concat_axis=0,
        tiled=True,
    )
    picked = returned.reshape(expert_total * capacity, model_width)[target].reshape(
        merged_count, TOP, model_width
    )
    weighted = jnp.zeros((merged_count, model_width), dtype=jnp.float32)
    for choice_index in range(TOP):
        weighted = weighted + gates[:, choice_index : choice_index + 1] * picked[
            :, choice_index
        ].astype(jnp.float32)
    expert_cols = lax.psum_scatter(
        weighted.astype(jnp.bfloat16), "section", scatter_dimension=1, tiled=True
    ).astype(jnp.float32)
    return (proj_own.astype(jnp.float32) + expert_cols).astype(jnp.bfloat16)


def solution(mesh):
    return jax.shard_map(
        per_device,
        mesh=mesh,
        in_specs=(
            P(("dp", "expert"), None),
            P(("dp", "expert"), None),
            P(None, "section"),
            P("section", None),
            P("dp", "section"),
            P(("dp", "expert"), None),
            P(("dp", "expert"), None),
            P(("dp", "expert"), None, "section"),
            P(("dp", "expert"), None, "section"),
            P(("dp", "expert"), "section", None),
        ),
        out_specs=P(("dp", "expert"), "section"),
        check_vma=False,
    )
```

profile of v0, /device:TPU:0, one launch (start us, length us, event | category | flops | bytes accessed | tf_op | source)
XLA Modules:
  0.0 499.0 jit_solution(13847764210738101677)
XLA Ops:
  7.4 0.0 copy-start
  7.4 0.0 all-reduce.2.cloned.1.call-start
  7.4 1.6 convert_reduce_fusion
  9.0 1.7 fusion.12
  10.8 0.8 reduce-window.18
  11.6 0.1 convert_reduce_fusion.1
  11.7 0.2 broadcast_compare_fusion
  11.9 6.4 %convolution_convert_fusion.1 = bf16[512,1728]{0,1:T(8,128)(2,1)} fusion(bf16[1152,1728]{0,1:T(8,128)(2,1)} %param.12, bf16[512,1152]{1,0:T(8,128)(2,1)} %param.10, f32[512]{0:T(512)S(1)} %add_rsqrt_fusion, f32[512]{0:T(512)S(1)} %broadcast_multiply_fusion.1), kind=kOutput, calls=%fused_computation.17 | convolution fusion | flops 2041675776 | bytes 6934528 | tf_op jit(solution)/shard_map/dot_general | solution.py:31
  18.3 8.0 %fusion.42 = (f32[8,512]{1,0:T(8,128)S(1)}, f32[8,512,512]{1,2,0:T(8,128)}) fusion(pred[512,512]{0,1:T(8,128)(4,1)S(1)} %broadcast_compare_fusion, bf16[512,8,3,72]{0,3,2,1:T(8,128)(2,1)} %bitcast.131), kind=kOutput, calls=%fused_computation.99 | convolution fusion | flops 312476160 | bytes 10108928 | tf_op jit(solution)/shard_map/while/body/eval_jaxpr/sub | solution.py:51
  26.4 0.0 copy-start.7
  26.4 4.5 fusion.15
  30.9 0.0 copy-done.7
  30.9 2.2 convolution_convert_fusion.2
  33.1 0.0 copy-start.4
  33.1 0.0 all-reduce.2.cloned.1.call-update
  33.2 0.0 all-gather.2.cloned.1.call-start
  33.2 0.5 all-gather.2.cloned.1.call-update
  33.7 0.1 copy-done.4
  33.8 0.1 copy.34
  33.9 0.1 eq.56
  34.1 0.1 eq.52
  34.2 1.7 reduce-window.19
  35.9 0.3 slice_reduce_fusion
  36.2 0.1 copy.33
  36.3 0.1 mul.135
  36.5 0.1 fusion.31
  36.6 3.6 scatter_custom_fusion
  40.2 38.7 %all-reduce.2.cloned.1.call-done = bf16[512,1152]{1,0:T(8,128)(2,1)} async-done(((bf16[512,1152]{1,0:T(8,128)(2,1)}), bf16[512,1152]{1,0:T(8,128)(2,1)}) %all-reduce.2.cloned.1.call-update) | async-done | bytes 1179664 | tf_op jit(solution)/shard_map/psum | solution.py:65
  78.9 2.9 fusion.14
  81.9 2.6 convert_element_type.114
  84.4 17.6 %all-gather.2.cloned.1.call-done = bf16[4608,1024]{1,0:T(8,128)(2,1)} async-done(((bf16[1152,1024]{1,0:T(8,128)(2,1)}), bf16[4608,1024]{1,0:T(8,128)(2,1)}) %all-gather.2.cloned.1.call-update) | async-done | bytes 9437200 | tf_op jit(solution)/shard_map/all_gather | solution.py:72
  102.1 5.4 %convolution_convert_fusion.3 = bf16[128,1024]{1,0:T(8,128)(2,1)S(1)} fusion(bf16[128,4608]{1,0:T(8,128)(2,1)} %convert_element_type.114, bf16[4608,1024]{1,0:T(8,128)(2,1)} %all-gather.2.cloned.1.call-done), kind=kOutput, calls=%fused_computation.31 | convolution fusion | flops 1208090624 | bytes 10878976 | tf_op jit(solution)/shard_map/dot_general | solution.py:71
  107.5 0.0 copy-start.2
  107.5 9.1 %all_gather.7 = bf16[128,2048]{1,0:T(8,128)(2,1)S(1)} all-gather(bf16[128,1024]{1,0:T(8,128)(2,1)S(1)} %convolution_convert_fusion.3), channel_id=1, replica_groups=mesh['section'=2,'dp'=4,'expert'=4] {'section'}, dimensions={1}, use_global_device_ids=true | all-gather | bytes 786432 | tf_op jit(solution)/shard_map/all_gather | solution.py:74
  116.7 0.2 fusion.19
  116.9 0.0 copy-done.2
  116.9 0.2 fusion.20
  117.1 7.1 %gather_fusion = bf16[1536,2048]{1,0:T(8,128)(2,1)} fusion(bf16[128,2048]{1,0:T(8,128)(2,1)S(1)} %fusion.20, s32[2048]{0:T(1024)S(1)} %pad_clamp_fusion), kind=kCustom, calls=%fused_computation | custom fusion | bytes 12589056 | tf_op jit(solution)/shard_map/gather | solution.py:88
  124.2 0.0 copy-start.6
  124.2 144.4 %all_to_all.10 = bf16[16,96,2048]{2,1,0:T(8,128)(2,1)S(1)} all-to-all(bf16[16,96,2048]{2,1,0:T(8,128)(2,1)} %bitcast.125), channel_id=1, replica_groups=mesh['section'=2,'dp'=4,'expert'=4] {'dp','expert'}, dimensions={0} | all-to-all | bytes 12582912 | tf_op jit(solution)/shard_map/all_to_all | solution.py:89
  268.6 0.0 copy-start.1
  268.6 2.7 copy-done.1
  271.2 0.0 copy-done.6
  271.2 6.2 %fusion.8 = f32[1536,704]{0,1:T(8,128)} fusion(bf16[1536,2048]{1,0:T(8,128)(2,1)S(1)} %bitcast.127, bf16[1,2048,704]{1,2,0:T(8,128)(2,1)S(1)} %copy-done.6), kind=kOutput, calls=%fused_computation.21 | convolution fusion | flops 4429185024 | bytes 13500416 | tf_op jit(solution)/shard_map/dot_general | solution.py:91
  277.5 0.0 copy-done
  277.5 18.2 %convolution_convert_fusion = bf16[1536,2048]{1,0:T(8,128)(2,1)} fusion(bf16[1,704,2048]{2,1,0:T(8,128)(2,1)S(1)} %copy-done, f32[1536,704]{0,1:T(8,128)} %fusion.8, bf16[1536,2048]{1,0:T(8,128)(2,1)} %bitcast.128, bf16[1,2048,704]{1,2,0:T(8,128)(2,1)} %param.18), kind=kOutput, calls=%fused_computation.7 | convolution fusion | flops 8868003840 | bytes 22675456 | tf_op jit(solution)/shard_map/dot_general | solution.py:94
  295.6 0.0 copy-start.5
  295.6 4.8 all-to-all-start.1
  300.4 0.3 reduce-scatter.2.cloned.1.call-start
  300.7 0.0 copy-done.5
  300.7 139.0 %all-to-all-done.1 = bf16[16,96,2048]{2,1,0:T(8,128)(2,1)} async-done(((bf16[16,96,2048]{2,1,0:T(8,128)(2,1)}), bf16[16,96,2048]{2,1,0:T(8,128)(2,1)}, u32[]{:S(2)}, u32[]{:S(2)}) %all-to-all-start.1) | async-done | bytes 6291488 | tf_op jit(solution)/shard_map/all_to_all | solution.py:95
  439.8 10.7 %gather_fusion.1 = bf16[768,2048]{1,0:T(8,128)(2,1)} fusion(bf16[1536,2048]{1,0:T(8,128)(2,1)} %bitcast.16, s32[1024]{0:T(1024)S(1)} %pad_clamp_fusion.1), kind=kCustom, calls=%fused_computation.1 | custom fusion | bytes 6294528 | tf_op jit(solution)/shard_map/gather | solution.py:102
  450.4 6.3 %reshape.176 = bf16[128,6,2048]{2,1,0:T(8,128)(2,1)} reshape(bf16[768,2048]{1,0:T(8,128)(2,1)} %gather_fusion.1) | data formatting | bytes 6291456 | tf_op jit(solution)/shard_map/reshape | solution.py:102
  456.7 15.6 %fusion.41 = (bf16[128,1,2048]{2,1,0:T(2,128)(2,1)S(1)}, bf16[128,1,2048]{2,1,0:T(2,128)(2,1)S(1)}, bf16[128,1,2048]{2,1,0:T(2,128)(2,1)S(1)}, bf16[128,1,2048]{...) fusion(bf16[128,6,2048]{2,1,0:T(8,128)(2,1)} %reshape.176), kind=kLoop, calls=%fused_computation.98 | loop fusion | bytes 6291456 | tf_op jit(solution)/shard_map/slice | solution.py:107
  472.3 0.0 copy-start.3
  472.3 4.2 fusion.22
  476.5 0.0 reduce-scatter.2.cloned.1.call-update
  476.5 13.3 %reduce-scatter.2.cloned.1.call-done = bf16[128,1024]{1,0:T(8,128)(2,1)} async-done(((bf16[128,2048]{1,0:T(8,128)(2,1)}), bf16[128,1024]{1,0:T(8,128)(2,1)}) %reduce-scatter.2.cloned.1.call-update) | async-done | bytes 262160 | tf_op jit(solution)/shard_map/reduce_scatter | solution.py:110
  489.8 0.0 copy-done.3
  489.8 1.7 add_convert_fusion
  (13 shorter events, 0.1 us)
Async XLA Ops:
  7.4 270.1 %copy-start = (bf16[1,704,2048]{2,1,0:T(8,128)(2,1)S(1)}, bf16[1,704,2048]{2,1,0:T(8,128)(2,1)}, u32[]{:S(2)}) copy-start(bf16[1,704,2048]{2,1,0:T(8,128)(2,1)} %param.19) | copy-start | bytes 8650756
  7.4 71.5 %all-reduce.2.cloned.1.call-start = ((), (), s32[]{:S(2)}) async-start(), calls=%async_computation.3 | async-start | bytes 2359296 | tf_op jit(solution)/shard_map/psum | solution.py:65
  26.4 4.5 copy-start.7
  33.1 0.7 copy-start.4
  33.2 68.9 %all-gather.2.cloned.1.call-start = ((), (), s32[]{:S(2)}) async-start(), calls=%async_computation.4 | async-start | bytes 11796480 | tf_op jit(solution)/shard_map/all_gather | solution.py:72
  107.5 9.3 %copy-start.2 = (bf16[128,1024]{1,0:T(8,128)(2,1)}, bf16[128,1024]{1,0:T(8,128)(2,1)S(1)}, u32[]{:S(2)}) copy-start(bf16[128,1024]{1,0:T(8,128)(2,1)S(1)} %convolution_convert_fusion.3) | copy-start | bytes 786436
  124.2 147.1 %copy-start.6 = (bf16[1,2048,704]{1,2,0:T(8,128)(2,1)S(1)}, bf16[1,2048,704]{1,2,0:T(8,128)(2,1)}, u32[]{:S(2)}) copy-start(bf16[1,2048,704]{1,2,0:T(8,128)(2,1)} %param.17) | copy-start | bytes 8650756
  268.6 2.7 copy-start.1
  295.6 5.1 %copy-start.5 = (f32[128,6]{0,1:T(8,128)S(1)}, f32[128,6]{0,1:T(8,128)}, u32[]{:S(2)}) copy-start(f32[128,6]{0,1:T(8,128)} %param.16) | copy-start | bytes 9220
  295.6 144.1 %all-to-all-start.1 = ((bf16[16,96,2048]{2,1,0:T(8,128)(2,1)}), bf16[16,96,2048]{2,1,0:T(8,128)(2,1)}, u32[]{:S(2)}, u32[]{:S(2)}) async-start(bf16[16,96,2048]{2,1,0:T(8,128)(2,1)} %bitcast.126), calls=%async_computation.1 | async-start | bytes 12582912 | tf_op jit(solution)/shard_map/all_to_all | solution.py:95
  300.4 189.4 %reduce-scatter.2.cloned.1.call-start = ((), (), s32[]{:S(2)}) async-start(), calls=%async_computation.5 | async-start | bytes 786432 | tf_op jit(solution)/shard_map/reduce_scatter | solution.py:110
  472.3 17.5 %copy-start.3 = (bf16[128,1024]{1,0:T(8,128)(2,1)S(1)}, bf16[128,1024]{1,0:T(8,128)(2,1)}, u32[]{:S(2)}) copy-start(bf16[128,1024]{1,0:T(8,128)(2,1)} %copy-done.2) | copy-start | bytes 786436
Sparse Core Ops, SparseCore 0:
  33.3 45.5 all-reduce.1
  476.7 13.1 reduce-scatter.1
Sparse Core Ops, SparseCore 1:
  35.3 66.8 all-gather.1
where the time goes:
time: 500 us; the launch traced here: 499 us
  waiting for transfers between devices  209 us (42%)
  blocking collectives  154 us (31%)
  matrix products  51 us (10%)
  local copies, waits for them, and re-layouts  49.4 us (10%)
  other arithmetic  15.6 us (3%)
  between operations  15 us (3%)
  starting transfers between devices  5.1 us (1%)
    all_to_all x1, blocking collectives, per_device(): lax.all_to_all(outgoing, ('dp', 'expert'), split_axis=0, concat_axis=0, t...  144 us
    all_to_all x1, waiting for transfers between devices, per_device(): lax.all_to_all(result.reshape(received.shape[:-1] + (w_down.shape[2],)),...  139 us
    psum x1, waiting for transfers between devices, per_device(): lax.psum(jnp.dot(attended, w_out, preferred_element_type=jnp.float32).ast...  38.7 us
    dot_general x1, matrix products, per_device(): jnp.dot(hidden, w_down[0], preferred_element_type=jnp.float32)  18.2 us
    all_gather x1, waiting for transfers between devices, per_device(): lax.all_gather(w_proj, 'dp', axis=0, tiled=True)  17.6 us
    slice x1, local copies, waits for them, and re-layouts, per_device(): picked[:, choice_index].astype(jnp.float32)  15.6 us
    reduce_scatter x1, waiting for transfers between devices, per_device(): lax.psum_scatter(weighted.astype(jnp.bfloat16), 'section', scatter_dimens...  13.3 us
    gather x1, local copies, waits for them, and re-layouts, per_device(): returned.reshape(expert_total * capacity, model_width)[target]  10.7 us
  transfers between devices with their start and end apart: 4, of which 4 were waited for; matrix products, arithmetic and copies ran while one was open for 2% of the time, Pallas kernels for 0%

commit v1 on v0

--- a/solution.py
+++ b/solution.py
@@ -18,6 +18,103 @@
 
 def rms_norm(values):
     return values * lax.rsqrt(jnp.mean(values * values, axis=-1, keepdims=True) + 1e-06)
+
+
+def dense_experts(proj_own, routes, gates, w_gate, w_up, w_down):
+    everyone = ("dp", "expert", "section")
+    sections = lax.axis_size("section")
+    groups = lax.axis_size("dp") * lax.axis_size("expert")
+    rows, part = proj_own.shape
+    own_expert = lax.axis_index("dp") * lax.axis_size("expert") + lax.axis_index("expert")
+    per_expert = jnp.sum(
+        jnp.where(
+            routes[:, :, None] == jnp.arange(groups, dtype=jnp.int32)[None, None, :],
+            gates[:, :, None],
+            0.0,
+        ),
+        axis=1,
+    )
+    weight = lax.all_gather(per_expert, ("dp", "expert"), axis=0, tiled=True)
+    weight = jnp.sum(
+        jnp.where(jnp.arange(groups, dtype=jnp.int32)[None, :] == own_expert, weight, 0.0),
+        axis=1,
+        keepdims=True,
+    )
+    tokens = lax.all_gather(proj_own, everyone, axis=0, tiled=False)
+    tokens = tokens.reshape(groups, sections, rows, part)
+    pieces = [tokens[:, q].reshape(groups * rows, part) for q in range(sections)]
+    squares = sum(
+        jnp.sum(jnp.square(piece.astype(jnp.float32)), axis=1, keepdims=True) for piece in pieces
+    )
+    inverse = lax.rsqrt(squares / (sections * part) + 1e-06)
+    gate_act = sum(
+        jnp.dot(
+            piece, w_gate[0, q * part : (q + 1) * part], preferred_element_type=jnp.float32
+        )
+        for q, piece in enumerate(pieces)
+    )
+    up_act = sum(
+        jnp.dot(piece, w_up[0, q * part : (q + 1) * part], preferred_element_type=jnp.float32)
+        for q, piece in enumerate(pieces)
+    )
+    hidden = (jax.nn.silu(gate_act * inverse) * (up_act * inverse)).astype(jnp.bfloat16)
+    sums = [
+        (
+            jnp.dot(
+                hidden, w_down[0, :, q * part : (q + 1) * part], preferred_element_type=jnp.float32
+            )
+            * weight
+        )
+        .astype(jnp.bfloat16)
+        .reshape(groups, rows, part)
+        for q in range(sections)
+    ]
+    shares = jnp.stack(sums, axis=1).reshape(groups * sections * rows, part)
+    total = lax.psum_scatter(shares, everyone, scatter_dimension=0, tiled=True)
+    return (proj_own.astype(jnp.float32) + total.astype(jnp.float32)).astype(jnp.bfloat16)
+
+
+def routed_experts(proj_own, routes, gates, w_gate, w_up, w_down, capacity):
+    projected = lax.all_gather(proj_own, "section", axis=1, tiled=True)
+    model_width = projected.shape[1]
+    normed_tokens = rms_norm(projected.astype(jnp.float32)).astype(jnp.bfloat16)
+    expert_total = lax.axis_size("dp") * lax.axis_size("expert")
+    merged_count = proj_own.shape[0]
+    route_flat = routes.reshape(-1)
+    onehot = (route_flat[:, None] == jnp.arange(expert_total, dtype=jnp.int32)[None, :]).astype(
+        jnp.int32
+    )
+    ranks = jnp.cumsum(onehot, axis=0) - 1
+    slots = jnp.sum(ranks * onehot, axis=1)
+    target = route_flat * capacity + slots
+    owners = jnp.arange(merged_count * TOP, dtype=jnp.int32) // TOP
+    source = jnp.zeros((expert_total * capacity,), dtype=jnp.int32).at[target].set(owners)
+    outgoing = normed_tokens[source].reshape(expert_total, capacity, model_width)
+    received = lax.all_to_all(outgoing, ("dp", "expert"), split_axis=0, concat_axis=0, tiled=True)
+    flat_rows = received.reshape(-1, received.shape[-1])
+    gate_act = jnp.dot(flat_rows, w_gate[0], preferred_element_type=jnp.float32)
+    up_act = jnp.dot(flat_rows, w_up[0], preferred_element_type=jnp.float32)
+    hidden = (jax.nn.silu(gate_act) * up_act).astype(jnp.bfloat16)
+    result = jnp.dot(hidden, w_down[0], preferred_element_type=jnp.float32).astype(jnp.bfloat16)
+    returned = lax.all_to_all(
+        result.reshape(received.shape[:-1] + (w_down.shape[2],)),
+        ("dp", "expert"),
+        split_axis=0,
+        concat_axis=0,
+        tiled=True,
+    )
+    picked = returned.reshape(expert_total * capacity, model_width)[target].reshape(
+        merged_count, TOP, model_width
+    )
+    weighted = jnp.zeros((merged_count, model_width), dtype=jnp.float32)
+    for choice_index in range(TOP):
+        weighted = weighted + gates[:, choice_index : choice_index + 1] * picked[
+            :, choice_index
+        ].astype(jnp.float32)
+    expert_cols = lax.psum_scatter(
+        weighted.astype(jnp.bfloat16), "section", scatter_dimension=1, tiled=True
+    ).astype(jnp.float32)
+    return (proj_own.astype(jnp.float32) + expert_cols).astype(jnp.bfloat16)
 
 
 def per_device(patches, lengths, w_qkv, w_out, w_proj, routes, gates, w_gate, w_up, w_down):
@@ -71,46 +168,11 @@
     proj_own = jnp.dot(
         merged, lax.all_gather(w_proj, "dp", axis=0, tiled=True), preferred_element_type=jnp.float32
     ).astype(jnp.bfloat16)
-    projected = lax.all_gather(proj_own, "section", axis=1, tiled=True)
-    model_width = projected.shape[1]
-    normed_tokens = rms_norm(projected.astype(jnp.float32)).astype(jnp.bfloat16)
     expert_total = data_count * owner_count
     capacity = max(2, min(merged_count, 2 * merged_count * TOP // expert_total))
-    route_flat = routes.reshape(-1)
-    onehot = (route_flat[:, None] == jnp.arange(expert_total, dtype=jnp.int32)[None, :]).astype(
-        jnp.int32
-    )
-    ranks = jnp.cumsum(onehot, axis=0) - 1
-    slots = jnp.sum(ranks * onehot, axis=1)
-    target = route_flat * capacity + slots
-    owners = jnp.arange(merged_count * TOP, dtype=jnp.int32) // TOP
-    source = jnp.zeros((expert_total * capacity,), dtype=jnp.int32).at[target].set(owners)
-    outgoing = normed_tokens[source].reshape(expert_total, capacity, model_width)
-    received = lax.all_to_all(outgoing, ("dp", "expert"), split_axis=0, concat_axis=0, tiled=True)
-    flat_rows = received.reshape(-1, received.shape[-1])
-    gate_act = jnp.dot(flat_rows, w_gate[0], preferred_element_type=jnp.float32)
-    up_act = jnp.dot(flat_rows, w_up[0], preferred_element_type=jnp.float32)
-    hidden = (jax.nn.silu(gate_act) * up_act).astype(jnp.bfloat16)
-    result = jnp.dot(hidden, w_down[0], preferred_element_type=jnp.float32).astype(jnp.bfloat16)
-    returned = lax.all_to_all(
-        result.reshape(received.shape[:-1] + (w_down.shape[2],)),
-        ("dp", "expert"),
-        split_axis=0,
-        concat_axis=0,
-        tiled=True,
-    )
-    picked = returned.reshape(expert_total * capacity, model_width)[target].reshape(
-        merged_count, TOP, model_width
-    )
-    weighted = jnp.zeros((merged_count, model_width), dtype=jnp.float32)
-    for choice_index in range(TOP):
-        weighted = weighted + gates[:, choice_index : choice_index + 1] * picked[
-            :, choice_index
-        ].astype(jnp.float32)
-    expert_cols = lax.psum_scatter(
-        weighted.astype(jnp.bfloat16), "section", scatter_dimension=1, tiled=True
-    ).astype(jnp.float32)
-    return (proj_own.astype(jnp.float32) + expert_cols).astype(jnp.bfloat16)
+    if merged_count <= 2 * capacity:
+        return dense_experts(proj_own, routes, gates, w_gate, w_up, w_down)
+    return routed_experts(proj_own, routes, gates, w_gate, w_up, w_down, capacity)
 
 
 def solution(mesh):

time: 500 us -> 422 us (0.84)
  blocking collectives: 154 us -> 33.2 us
  waiting for transfers between devices: 209 us -> 293 us
  local copies, waits for them, and re-layouts: 49.4 us -> 4.98 us
  matrix products: 51 us -> 56.2 us
    reduce_scatter x1, waiting for transfers between devices: 13.3 us -> 184 us  [dense_experts(): total = lax.psum_scatter(shares, everyone, scatter_dimension=0, tiled=True)]
    all_to_all x1 -> x0, blocking collectives: 144 us -> none  [per_device(): lax.all_to_all(outgoing, ('dp', 'expert'), split_axis=0, concat_axis=0, t...]
    all_to_all x1 -> x0, waiting for transfers between devices: 139 us -> none  [per_device(): lax.all_to_all(result.reshape(received.shape[:-1] + (w_down.shape[2],)),...]
    all_gather x0 -> x1, waiting for transfers between devices: none -> 44.5 us  [dense_experts(): tokens = lax.all_gather(proj_own, everyone, axis=0, tiled=False)]
    all_gather x1, blocking collectives: 9.15 us -> 33.2 us  [dense_experts(): weight = lax.all_gather(per_expert, ('dp', 'expert'), axis=0, tiled=True)]
    gather x2 -> x0, local copies, waits for them, and re-layouts: 17.8 us -> none  [the longest x1 10.7 us: per_device(): returned.reshape(expert_total * capacity, model_width)[target]]
    slice x2 -> x1, local copies, waits for them, and re-layouts: 15.9 us -> 1 us  [dense_experts(): tokens[:, q].reshape(groups * rows, part)]
    dot_general x2 -> x6, matrix products: 24.4 us -> 33 us  [the longest x2 11.9 us: dense_experts(): jnp.dot(piece, w_up[0, q * part:(q + 1) * part], preferred_element_type=j...]
  transfers between devices with their start and end apart: 4 -> 4, of which waited for: 4 -> 4; matrix products, arithmetic and copies ran while one was open for 2% -> 1% of each run, Pallas kernels for 0% -> 0%
where the time goes in v1:
time: 422 us; the launch traced here: 421 us
  waiting for transfers between devices  293 us (69%)
  matrix products  56.2 us (13%)
  blocking collectives  33.2 us (8%)
  other arithmetic  19.6 us (5%)
  between operations  14.7 us (3%)
  local copies, waits for them, and re-layouts  4.98 us (1%)
    reduce_scatter x1, waiting for transfers between devices, dense_experts(): total = lax.psum_scatter(shares, everyone, scatter_dimension=0, tiled=True)  184 us
    psum x1, waiting for transfers between devices, per_device(): lax.psum(jnp.dot(attended, w_out, preferred_element_type=jnp.float32).ast...  45.1 us
    all_gather x1, waiting for transfers between devices, dense_experts(): tokens = lax.all_gather(proj_own, everyone, axis=0, tiled=False)  44.5 us
    all_gather x1, blocking collectives, dense_experts(): weight = lax.all_gather(per_expert, ('dp', 'expert'), axis=0, tiled=True)  33.2 us
    all_gather x1, waiting for transfers between devices, per_device(): lax.all_gather(w_proj, 'dp', axis=0, tiled=True)  18.7 us
    dot_general x2, matrix products, dense_experts(): jnp.dot(piece, w_up[0, q * part:(q + 1) * part], preferred_element_type=j...  11.9 us
    dot_general x2, matrix products, dense_experts(): jnp.dot(hidden, w_down[0, :, q * part:(q + 1) * part], preferred_element_...  11.1 us
    dot_general x2, matrix products, dense_experts(): jnp.dot(piece, w_gate[0, q * part:(q + 1) * part], preferred_element_type...  10.1 us
  transfers between devices with their start and end apart: 4, of which 4 were waited for; matrix products, arithmetic and copies ran while one was open for 1% of the time, Pallas kernels for 0%

profile of v1, /device:TPU:0, one launch (start us, length us, event | category | flops | bytes accessed | tf_op | source)
XLA Modules:
  0.0 421.5 jit_solution(4449725697934852321)
XLA Ops:
  7.4 0.0 copy-start
  7.4 0.0 all-reduce.2.cloned.1.call-start
  7.4 0.9 reduce-window.8
  8.3 0.1 convert_reduce_fusion.1
  8.4 1.5 convert_reduce_fusion
  9.9 1.7 fusion.8
  11.6 0.2 broadcast_compare_fusion
  11.9 5.1 %convolution_convert_fusion = bf16[512,1728]{0,1:T(8,128)(2,1)S(1)} fusion(bf16[1152,1728]{0,1:T(8,128)(2,1)} %param.12, bf16[512,1152]{1,0:T(8,128)(2,1)} %param.10, f32[512]{0:T(512)S(1)} %add_rsqrt_fusion, f32[512]{0:T(512)S(1)} %broadcast_multiply_fusion), kind=kOutput, calls=%fused_computation.18 | convolution fusion | flops 2041675776 | bytes 6934528 | tf_op jit(solution)/shard_map/dot_general | solution.py:128
  17.0 5.8 %fusion.36 = (f32[8,512]{1,0:T(8,128)S(1)}, f32[8,512,512]{1,2,0:T(8,128)}) fusion(pred[512,512]{0,1:T(8,128)(4,1)S(1)} %broadcast_compare_fusion, bf16[512,8,3,72]{0,3,2,1:T(8,128)(2,1)S(1)} %bitcast.89), kind=kOutput, calls=%fused_computation.64 | convolution fusion | flops 312476160 | bytes 10108928 | tf_op jit(solution)/shard_map/while/body/eval_jaxpr/sub | solution.py:148
  22.8 4.2 %fusion.26 = bf16[8,72,512]{2,1,0:T(8,128)(2,1)S(1)} fusion(f32[8,512,512]{1,2,0:T(8,128)} %get-tuple-element.30, f32[8,512]{1,0:T(8,128)S(1)} %get-tuple-element.28, bf16[512,8,3,72]{0,3,2,1:T(8,128)(2,1)S(1)} %bitcast.90), kind=kOutput, calls=%fused_computation.40 | convolution fusion | flops 306479104 | bytes 9584640 | tf_op jit(solution)/shard_map/while/body/eval_jaxpr/hqk,khd->qhd/dot_general | solution.py:150
  27.0 0.0 copy-done
  27.0 0.0 copy-start.3
  27.0 2.2 convolution_convert_fusion.1
  29.3 0.0 all-reduce.2.cloned.1.call-update
  29.3 0.0 all-gather.4.cloned.1.call-start
  29.3 0.5 all-gather.4.cloned.1.call-update
  29.9 0.0 all-gather.6.cloned.1.call-start
  29.9 45.1 %all-reduce.2.cloned.1.call-done = bf16[512,1152]{1,0:T(8,128)(2,1)} async-done(((bf16[512,1152]{1,0:T(8,128)(2,1)}), bf16[512,1152]{1,0:T(8,128)(2,1)}) %all-reduce.2.cloned.1.call-update) | async-done | bytes 1179664 | tf_op jit(solution)/shard_map/psum | solution.py:162
  75.0 0.0 copy-done.3
  75.1 2.6 fusion.10
  77.6 1.8 convert_element_type.75
  79.4 0.0 copy-start.5
  79.5 0.0 copy-start.6
  79.5 18.7 %all-gather.4.cloned.1.call-done = bf16[4608,1024]{1,0:T(8,128)(2,1)} async-done(((bf16[1152,1024]{1,0:T(8,128)(2,1)}), bf16[4608,1024]{1,0:T(8,128)(2,1)}) %all-gather.4.cloned.1.call-update) | async-done | bytes 9437200 | tf_op jit(solution)/shard_map/all_gather | solution.py:169
  98.2 5.8 %convolution_convert_fusion.2 = bf16[128,1024]{1,0:T(8,128)(2,1)} fusion(bf16[128,4608]{1,0:T(8,128)(2,1)S(1)} %convert_element_type.75, bf16[4608,1024]{1,0:T(8,128)(2,1)} %all-gather.4.cloned.1.call-done), kind=kOutput, calls=%fused_computation.41 | convolution fusion | flops 1208090624 | bytes 10878976 | tf_op jit(solution)/shard_map/dot_general | solution.py:168
  104.0 0.0 all-gather.6.cloned.1.call-update
  104.0 0.0 reduce-scatter.2.cloned.1.call-start
  104.1 0.0 copy-done.5
  104.1 0.0 copy-done.6
  104.1 33.2 %all_gather.15 = f32[2048,16]{0,1:T(8,128)S(1)} all-gather(f32[128,16]{0,1:T(8,128)S(1)} %select_reduce_fusion.1), channel_id=1, replica_groups=mesh['section'=2,'dp'=4,'expert'=4] {'dp','expert'}, dimensions={0}, use_global_device_ids=true | all-gather | bytes 139264 | tf_op jit(solution)/shard_map/all_gather | solution.py:37
  137.3 0.1 select_reduce_fusion
  137.4 44.5 %all-gather.6.cloned.1.call-done = bf16[4096,1024]{1,0:T(8,128)(2,1)} async-done(((bf16[128,1024]{1,0:T(8,128)(2,1)}), bf16[4096,1024]{1,0:T(8,128)(2,1)}) %all-gather.6.cloned.1.call-update) | async-done | bytes 8388624 | tf_op jit(solution)/shard_map/all_gather | solution.py:43
  181.9 0.0 copy-start.2
  181.9 4.5 %multiply_reduce_fusion = (f32[16,128]{1,0:T(8,128)S(1)}, f32[16,128]{1,0:T(8,128)S(1)}) fusion(bf16[16,2,128,1024]{3,2,1,0:T(8,128)(2,1)} %bitcast.79), kind=kLoop, calls=%fused_computation.4 | loop fusion | flops 12578816 | bytes 8404992 | tf_op jit(solution)/shard_map/reduce_sum | solution.py:47
  186.4 1.3 copy-done.2
  187.7 0.0 copy-start.8
  187.7 1.0 fusion.35
  188.8 0.8 copy-done.8
  189.6 0.0 copy-start.7
  189.6 3.2 fusion.14
  192.7 0.0 copy-done.7
  192.8 5.0 %fusion.18 = f32[2048,704]{0,1:T(8,128)} fusion(bf16[2048,1024]{1,0:T(8,128)(2,1)S(1)} %bitcast.85, bf16[1,2048,704]{1,2,0:T(8,128)(2,1)S(1)} %copy-done.7), kind=kOutput, calls=%fused_computation.32 | convolution fusion | flops 2952790016 | bytes 11403264 | tf_op jit(solution)/shard_map/dot_general | solution.py:51
  197.8 5.1 %fusion.16 = f32[2048,704]{0,1:T(8,128)} fusion(bf16[2048,1024]{1,0:T(8,128)(2,1)S(1)} %bitcast.82, bf16[1,2048,704]{1,2,0:T(8,128)(2,1)S(1)} %copy-done.7), kind=kOutput, calls=%fused_computation.30 | convolution fusion | flops 2952790016 | bytes 11403264 | tf_op jit(solution)/shard_map/dot_general | solution.py:51
  202.9 0.0 copy-start.9
  202.9 8.7 %multiply_convert_fusion.2 = bf16[2048,704]{0,1:T(8,128)(2,1)} fusion(f32[2048,704]{0,1:T(8,128)S(1)} %fusion.14, f32[2048,704]{0,1:T(8,128)} %fusion.18, f32[2048,704]{0,1:T(8,128)} %fusion.16, bf16[2048,1024]{1,0:T(8,128)(2,1)S(1)} %bitcast.83, f32[2048]{0:T(1024)S(1)} %rsqrt_bitcast_fusion, bf16[1,2048,704]{1,2,0:T(8,128)(2,1)S(1)} %copy-done.8), kind=kOutput, calls=%fused_computation.10 | convolution fusion | flops 2967207936 | bytes 25829376 | tf_op jit(solution)/shard_map/dot_general | solution.py:57
  211.6 0.0 copy-done.9
  211.6 0.0 copy-start.10
  211.6 5.7 %multiply_convert_fusion = bf16[2048,1024]{1,0:T(8,128)(2,1)S(1)} fusion(bf16[2048,704]{0,1:T(8,128)(2,1)} %multiply_convert_fusion.2, f32[2048]{0:T(1024)S(1)} %select_reduce_fusion, bf16[1,704,2048]{2,1,0:T(8,128)(2,1)S(1)} %copy-done.9), kind=kOutput, calls=%fused_computation.2 | convolution fusion | flops 2956984320 | bytes 8527872 | tf_op jit(solution)/shard_map/dot_general | solution.py:63
  217.3 0.0 copy-done.10
  217.3 5.4 %multiply_convert_fusion.1 = bf16[2048,1024]{1,0:T(8,128)(2,1)} fusion(bf16[2048,704]{0,1:T(8,128)(2,1)S(1)} %copy-done.10, f32[2048]{0:T(1024)S(1)} %select_reduce_fusion, bf16[1,704,2048]{2,1,0:T(8,128)(2,1)S(1)} %copy-done.9), kind=kOutput, calls=%fused_computation.3 | convolution fusion | flops 2956984320 | bytes 8527872 | tf_op jit(solution)/shard_map/dot_general | solution.py:63
  222.7 6.2 %pad_maximum_fusion = bf16[16,2,128,1024]{3,2,1,0:T(8,128)(2,1)} fusion(bf16[16,1,128,1024]{3,2,1,0:T(8,128)(2,1)S(1)} %bitcast.86, bf16[16,1,128,1024]{3,2,1,0:T(8,128)(2,1)} %bitcast.87), kind=kLoop, calls=%fused_computation.1 | loop fusion | flops 4194304 | bytes 16777216 | tf_op jit(solution)/shard_map/stack | solution.py:72
  228.8 0.0 copy-start.1
  228.8 0.0 copy-start.4
  228.8 0.0 reduce-scatter.2.cloned.1.call-update
  228.9 183.7 %reduce-scatter.2.cloned.1.call-done = bf16[128,1024]{1,0:T(8,128)(2,1)} async-done(((bf16[4096,1024]{1,0:T(8,128)(2,1)}), bf16[128,1024]{1,0:T(8,128)(2,1)}) %reduce-scatter.2.cloned.1.call-update) | async-done | bytes 262160 | tf_op jit(solution)/shard_map/reduce_scatter | solution.py:73
  412.6 0.0 copy-done.4
  412.6 1.7 add_convert_fusion
  414.3 0.0 copy-done.1
  (6 shorter events, 0.0 us)
Async XLA Ops:
  7.4 19.6 %copy-start = (bf16[576,1152]{1,0:T(8,128)(2,1)S(1)}, bf16[576,1152]{1,0:T(8,128)(2,1)}, u32[]{:S(2)}) copy-start(bf16[576,1152]{1,0:T(8,128)(2,1)} %param.13) | copy-start | bytes 3981316
  7.4 67.7 %all-reduce.2.cloned.1.call-start = ((), (), s32[]{:S(2)}) async-start(), calls=%async_computation.1 | async-start | bytes 2359296 | tf_op jit(solution)/shard_map/psum | solution.py:162
  27.0 48.0 %copy-start.3 = (bf16[512,1152]{1,0:T(8,128)(2,1)S(1)}, bf16[512,1152]{1,0:T(8,128)(2,1)}, u32[]{:S(2)}) copy-start(bf16[512,1152]{1,0:T(8,128)(2,1)} %param.10) | copy-start | bytes 3538948
  29.3 68.9 %all-gather.4.cloned.1.call-start = ((), (), s32[]{:S(2)}) async-start(), calls=%async_computation.2 | async-start | bytes 11796480 | tf_op jit(solution)/shard_map/all_gather | solution.py:169
  29.9 152.0 %all-gather.6.cloned.1.call-start = ((), (), s32[]{:S(2)}) async-start(), calls=%async_computation.4 | async-start | bytes 8650752 | tf_op jit(solution)/shard_map/all_gather | solution.py:43
  79.4 24.6 %copy-start.5 = (f32[128,6]{0,1:T(8,128)S(1)}, f32[128,6]{0,1:T(8,128)}, u32[]{:S(2)}) copy-start(f32[128,6]{0,1:T(8,128)} %param.16) | copy-start | bytes 9220
  79.5 24.6 %copy-start.6 = (s32[128,6]{0,1:T(8,128)S(1)}, s32[128,6]{0,1:T(8,128)}, u32[]{:S(2)}) copy-start(s32[128,6]{0,1:T(8,128)} %param.15) | copy-start | bytes 9220
  104.0 308.6 %reduce-scatter.2.cloned.1.call-start = ((), (), s32[]{:S(2)}) async-start(), calls=%async_computation.3 | async-start | bytes 8650752 | tf_op jit(solution)/shard_map/reduce_scatter | solution.py:73
  181.9 5.8 %copy-start.2 = (bf16[4096,1024]{1,0:T(8,128)(2,1)S(1)}, bf16[4096,1024]{1,0:T(8,128)(2,1)}, u32[]{:S(2)}) copy-start(bf16[4096,1024]{1,0:T(8,128)(2,1)} %all-gather.6.cloned.1.call-done) | copy-start | bytes 25165828
  187.7 1.8 copy-start.8
  189.6 3.2 copy-start.7
  202.9 8.7 %copy-start.9 = (bf16[1,704,2048]{2,1,0:T(8,128)(2,1)S(1)}, bf16[1,704,2048]{2,1,0:T(8,128)(2,1)}, u32[]{:S(2)}) copy-start(bf16[1,704,2048]{2,1,0:T(8,128)(2,1)} %param.19) | copy-start | bytes 8650756
  211.6 5.7 %copy-start.10 = (bf16[2048,704]{0,1:T(8,128)(2,1)S(1)}, bf16[2048,704]{0,1:T(8,128)(2,1)}, u32[]{:S(2)}) copy-start(bf16[2048,704]{0,1:T(8,128)(2,1)} %multiply_convert_fusion.2) | copy-start | bytes 8650756
  228.8 185.5 %copy-start.1 = (bf16[576,1152]{1,0:T(8,128)(2,1)S(1)}, bf16[576,1152]{1,0:T(8,128)(2,1)}, u32[]{:S(2)}) copy-start(bf16[576,1152]{1,0:T(8,128)(2,1)} %param.13) | copy-start | bytes 3981316
  228.8 183.8 %copy-start.4 = (bf16[128,1024]{1,0:T(8,128)(2,1)S(1)}, bf16[128,1024]{1,0:T(8,128)(2,1)}, u32[]{:S(2)}) copy-start(bf16[128,1024]{1,0:T(8,128)(2,1)} %convolution_convert_fusion.2) | copy-start | bytes 786436
Sparse Core Ops, SparseCore 0:
  29.4 45.5 all-reduce.1
  104.1 77.7 all-gather.5
  229.0 183.5 reduce-scatter.1
Sparse Core Ops, SparseCore 1:
  31.4 66.8 all-gather.3

commit v2 on v1

--- a/solution.py
+++ b/solution.py
@@ -20,12 +20,31 @@
     return values * lax.rsqrt(jnp.mean(values * values, axis=-1, keepdims=True) + 1e-06)
 
 
+def swapped(values, axis, bit):
+    count = lax.axis_size(axis)
+    return lax.ppermute(values, axis, [(i, i ^ bit) for i in range(count)])
+
+
+def halves(values):
+    high = lax.reduce_precision(values, 8, 7)
+    return [high.astype(jnp.bfloat16), (values - high).astype(jnp.bfloat16)]
+
+
+def pair_sum(own, other):
+    return (own.astype(jnp.float32) + other.astype(jnp.float32)).astype(jnp.bfloat16)
+
+
+def pick(values, index, axis):
+    return lax.dynamic_index_in_dim(values, index, axis, keepdims=False)
+
+
 def dense_experts(proj_own, routes, gates, w_gate, w_up, w_down):
-    everyone = ("dp", "expert", "section")
     sections = lax.axis_size("section")
-    groups = lax.axis_size("dp") * lax.axis_size("expert")
+    data_count = lax.axis_size("dp")
+    owners = lax.axis_size("expert")
+    groups = data_count * owners
     rows, part = proj_own.shape
-    own_expert = lax.axis_index("dp") * lax.axis_size("expert") + lax.axis_index("expert")
+    me_d, me_e, me_s = lax.axis_index("dp"), lax.axis_index("expert"), lax.axis_index("section")
     per_expert = jnp.sum(
         jnp.where(
             routes[:, :, None] == jnp.arange(groups, dtype=jnp.int32)[None, None, :],
@@ -34,44 +53,80 @@
         ),
         axis=1,
     )
-    weight = lax.all_gather(per_expert, ("dp", "expert"), axis=0, tiled=True)
-    weight = jnp.sum(
-        jnp.where(jnp.arange(groups, dtype=jnp.int32)[None, :] == own_expert, weight, 0.0),
-        axis=1,
-        keepdims=True,
-    )
-    tokens = lax.all_gather(proj_own, everyone, axis=0, tiled=False)
-    tokens = tokens.reshape(groups, sections, rows, part)
-    pieces = [tokens[:, q].reshape(groups * rows, part) for q in range(sections)]
-    squares = sum(
-        jnp.sum(jnp.square(piece.astype(jnp.float32)), axis=1, keepdims=True) for piece in pieces
-    )
-    inverse = lax.rsqrt(squares / (sections * part) + 1e-06)
-    gate_act = sum(
-        jnp.dot(
-            piece, w_gate[0, q * part : (q + 1) * part], preferred_element_type=jnp.float32
-        )
-        for q, piece in enumerate(pieces)
-    )
-    up_act = sum(
-        jnp.dot(piece, w_up[0, q * part : (q + 1) * part], preferred_element_type=jnp.float32)
-        for q, piece in enumerate(pieces)
-    )
-    hidden = (jax.nn.silu(gate_act * inverse) * (up_act * inverse)).astype(jnp.bfloat16)
-    sums = [
-        (
-            jnp.dot(
-                hidden, w_down[0, :, q * part : (q + 1) * part], preferred_element_type=jnp.float32
+    own = proj_own.astype(jnp.float32)
+    side = halves(per_expert) + halves(jnp.sum(own * own, axis=1, keepdims=True))
+    side = jnp.concatenate(side, axis=1)
+    side_width = -(-side.shape[1] // 128) * 128
+    side = jnp.pad(side, ((0, 0), (0, side_width - side.shape[1])))
+    sent = jnp.concatenate([proj_own, side], axis=1)
+    gathered = lax.all_gather(sent, ("dp", "expert", "section"), axis=0, tiled=False)
+    gathered = gathered.reshape(data_count, owners, sections, rows, part + side_width)
+    down = [
+        lax.dynamic_slice_in_dim(w_down[0], (me_s ^ flip) * part, part, axis=1)
+        for flip in range(sections)
+    ]
+    own_expert = me_d * owners + me_e
+    at_expert = jnp.arange(groups, dtype=jnp.int32)[None, :] == own_expert
+
+    def run(flip_d):
+        block = pick(gathered, me_d ^ flip_d, 0)
+        block = [block[:, q].reshape(owners * rows, part + side_width) for q in range(sections)]
+        tokens = [piece[:, :part] for piece in block]
+        sides = [piece[:, part:].astype(jnp.float32) for piece in block]
+        weight = sides[0][:, :groups] + sides[0][:, groups : 2 * groups]
+        weight = jnp.sum(jnp.where(at_expert, weight, 0.0), axis=1, keepdims=True)
+        squares = sum(
+            piece[:, 2 * groups : 2 * groups + 1] + piece[:, 2 * groups + 1 : 2 * groups + 2]
+            for piece in sides
+        )
+        inverse = lax.rsqrt(squares / (sections * part) + 1e-06)
+
+        def through(matrix):
+            product = sum(
+                jnp.dot(
+                    piece,
+                    matrix[0, q * part : (q + 1) * part],
+                    preferred_element_type=jnp.float32,
+                )
+                for q, piece in enumerate(tokens)
             )
-            * weight
-        )
-        .astype(jnp.bfloat16)
-        .reshape(groups, rows, part)
-        for q in range(sections)
-    ]
-    shares = jnp.stack(sums, axis=1).reshape(groups * sections * rows, part)
-    total = lax.psum_scatter(shares, everyone, scatter_dimension=0, tiled=True)
-    return (proj_own.astype(jnp.float32) + total.astype(jnp.float32)).astype(jnp.bfloat16)
+            return product * inverse
+
+        hidden = (jax.nn.silu(through(w_gate)) * through(w_up)).astype(jnp.bfloat16)
+        return [
+            (jnp.dot(hidden, piece, preferred_element_type=jnp.float32) * weight).astype(
+                jnp.bfloat16
+            )
+            for piece in down
+        ]
+
+    partial = {flip: run(flip) for flip in sorted(range(data_count), key=lambda f: (-(f & 1), -f))}
+    near = {}
+    for flip in range(data_count - 2, -1, -2):
+        near[flip] = [
+            pair_sum(partial[flip][q], swapped(partial[flip + 1][q], "dp", 1))
+            for q in range(sections)
+        ]
+    half = part // 2
+    left = [piece[:, :half] for piece in near[0]], [piece[:, :half] for piece in near[2]]
+    right = [piece[:, half:] for piece in near[0]], [piece[:, half:] for piece in near[2]]
+    far_left = pair_sum(left[1][0], swapped(left[1][1], "section", 1))
+    far_right = pair_sum(right[0][1], swapped(right[1][1], "dp", 2))
+    mid_left = pair_sum(left[0][0], swapped(left[0][1], "section", 1))
+    mid_right = pair_sum(right[0][0], swapped(right[1][0], "dp", 2))
+    mid_left = pair_sum(mid_left, swapped(far_left, "dp", 2))
+    mid_right = pair_sum(mid_right, swapped(far_right, "section", 1))
+    ends = []
+    for piece in (mid_left, mid_right):
+        piece = piece.reshape(owners // 2, 2, rows, half)
+        low = me_e & 1
+        piece = pair_sum(pick(piece, low, 1), swapped(pick(piece, 1 - low, 1), "expert", 1))
+        high = me_e // 2
+        ends.append(
+            pick(piece, high, 0).astype(jnp.float32)
+            + swapped(pick(piece, 1 - high, 0), "expert", 2).astype(jnp.float32)
+        )
+    return (own + jnp.concatenate(ends, axis=1)).astype(jnp.bfloat16)
 
 
 def routed_experts(proj_own, routes, gates, w_gate, w_up, w_down, capacity):
@@ -124,6 +179,11 @@
     head_dim = D_VIT // HEADS
     local_heads = w_qkv.shape[1] // (3 * head_dim)
     scale = 1.0 / math.sqrt(head_dim)
+    shards = [(0, w_proj)]
+    bit = data_count // 2
+    while bit >= 1:
+        shards = shards + [(flip ^ bit, swapped(shard, "dp", bit)) for flip, shard in shards]
+        bit //= 2
     normed_in = layer_norm(patches.astype(jnp.float32)).astype(jnp.bfloat16)
     packed = jnp.dot(normed_in, w_qkv, preferred_element_type=jnp.float32).astype(jnp.bfloat16)
     packed = packed.reshape(patch_rows, local_heads, 3, head_dim)
@@ -159,18 +219,28 @@
     )
     attended = attended.reshape(patch_rows, local_heads * head_dim)
     merged_count = patch_rows // 4
-    summed = lax.psum(
-        jnp.dot(attended, w_out, preferred_element_type=jnp.float32).astype(jnp.bfloat16), "section"
-    ).astype(jnp.float32)
+    mixed = jnp.dot(attended, w_out, preferred_element_type=jnp.float32).astype(jnp.bfloat16)
+    if lax.axis_size("section") == 2:
+        summed = mixed.astype(jnp.float32) + swapped(mixed, "section", 1).astype(jnp.float32)
+    else:
+        summed = lax.psum(mixed, "section").astype(jnp.float32)
     merged = (
         (patches.astype(jnp.float32) + summed).reshape(merged_count, 4 * width).astype(jnp.bfloat16)
     )
-    proj_own = jnp.dot(
-        merged, lax.all_gather(w_proj, "dp", axis=0, tiled=True), preferred_element_type=jnp.float32
+    depth = w_proj.shape[0]
+    me_d = lax.axis_index("dp")
+    proj_own = sum(
+        jnp.dot(
+            lax.dynamic_slice_in_dim(merged, (me_d ^ flip) * depth, depth, axis=1),
+            shard,
+            preferred_element_type=jnp.float32,
+        )
+        for flip, shard in shards
     ).astype(jnp.bfloat16)
     expert_total = data_count * owner_count
     capacity = max(2, min(merged_count, 2 * merged_count * TOP // expert_total))
-    if merged_count <= 2 * capacity:
+    shape = (lax.axis_size("section"), data_count, owner_count)
+    if shape == (2, 4, 4) and merged_count <= 2 * capacity:
         return dense_experts(proj_own, routes, gates, w_gate, w_up, w_down)
     return routed_experts(proj_own, routes, gates, w_gate, w_up, w_down, capacity)
 

time: 422 us -> 308 us (0.73)
  waiting for transfers between devices: 293 us -> 152 us
  blocking collectives: 33.2 us -> 0 us
  local copies, waits for them, and re-layouts: 4.98 us -> 26.8 us
  matrix products: 56.2 us -> 75.1 us
  starting transfers between devices: 0.13 us -> 17.6 us
    reduce_scatter x1 -> x0, waiting for transfers between devices: 184 us -> none  [dense_experts(): total = lax.psum_scatter(shares, everyone, scatter_dimension=0, tiled=True)]
    ppermute x0 -> x18, waiting for transfers between devices: none -> 68.2 us  [swapped(): return lax.ppermute(values, axis, [(i, i ^ bit) for i in range(count)])]
    psum x1 -> x0, waiting for transfers between devices: 45.1 us -> none  [per_device(): lax.psum(jnp.dot(attended, w_out, preferred_element_type=jnp.float32).ast...]
    all_gather x1 -> x0, blocking collectives: 33.2 us -> none  [dense_experts(): weight = lax.all_gather(per_expert, ('dp', 'expert'), axis=0, tiled=True)]
    all_gather x2 -> x1, waiting for transfers between devices: 63.3 us -> 83.7 us  [dense_experts(): lax.all_gather(sent, ('dp', 'expert', 'section'), axis=0, tiled=False)]
    ppermute x0 -> x18, starting transfers between devices: none -> 17.6 us  [swapped(): return lax.ppermute(values, axis, [(i, i ^ bit) for i in range(count)])]
    dot_general x7 -> x28, matrix products: 38.8 us -> 53.9 us  [the longest x16 29.7 us: through(): jnp.dot(piece, matrix[0, q * part:(q + 1) * part], preferred_element_type...]
    slice x1 -> x13, local copies, waits for them, and re-layouts: 1 us -> 11.1 us  [the longest x8 5.66 us: run(): sides = [piece[:, part:].astype(jnp.float32) for piece in block]]
  transfers between devices with their start and end apart: 4 -> 19, of which waited for: 4 -> 10; matrix products, arithmetic and copies ran while one was open for 1% -> 19% of each run, Pallas kernels for 0% -> 0%
where the time goes in v2:
time: 308 us; the launch traced here: 307 us
  waiting for transfers between devices  152 us (49%)
  matrix products  75.1 us (24%)
  local copies, waits for them, and re-layouts  26.8 us (9%)
  other arithmetic  21.3 us (7%)
  starting transfers between devices  17.6 us (6%)
  between operations  14 us (5%)
    all_gather x1, waiting for transfers between devices, dense_experts(): lax.all_gather(sent, ('dp', 'expert', 'section'), axis=0, tiled=False)  83.7 us
    ppermute x18, waiting for transfers between devices, swapped(): return lax.ppermute(values, axis, [(i, i ^ bit) for i in range(count)])  68.2 us
    dot_general x16, matrix products, through(): jnp.dot(piece, matrix[0, q * part:(q + 1) * part], preferred_element_type...  29.7 us
    ppermute x18, starting transfers between devices, swapped(): return lax.ppermute(values, axis, [(i, i ^ bit) for i in range(count)])  17.6 us
    dot_general x8, matrix products, run(): jnp.dot(hidden, piece, preferred_element_type=jnp.float32) * weight  15.1 us
    dot_general x4, matrix products, per_device(): jnp.dot(lax.dynamic_slice_in_dim(merged, (me_d ^ flip) * depth, depth, ax...  9.14 us
    sub x1, matrix products, attend(): weights = jnp.where(same[None], jnp.exp(scores - peak), 0.0)  8.07 us
    unnamed x64, local copies, waits for them, and re-layouts  7.2 us
  transfers between devices with their start and end apart: 19, of which 10 were waited for; matrix products, arithmetic and copies ran while one was open for 19% of the time, Pallas kernels for 0%

profile of v2, /device:TPU:0, one launch (start us, length us, event | category | flops | bytes accessed | tf_op | source)
XLA Modules:
  0.0 306.8 jit_solution(10102861579794264413)
XLA Ops:
  6.5 3.0 collective-permute-start.1
  9.6 1.5 convert_reduce_fusion
  12.1 6.4 %convolution_convert_fusion = bf16[512,1728]{0,1:T(8,128)(2,1)} fusion(bf16[1152,1728]{0,1:T(8,128)(2,1)} %param.12, bf16[512,1152]{1,0:T(8,128)(2,1)} %param.10, f32[512]{0:T(512)S(1)} %add_rsqrt_fusion.4, f32[512]{0:T(512)S(1)} %broadcast_multiply_fusion), kind=kOutput, calls=%fused_computation.12 | convolution fusion | flops 2041675776 | bytes 6934528 | tf_op jit(solution)/shard_map/dot_general | solution.py:188
  18.4 8.1 %fusion.169 = (f32[8,512]{1,0:T(8,128)S(1)}, f32[8,512,512]{1,2,0:T(8,128)}) fusion(pred[512,512]{0,1:T(8,128)(4,1)S(1)} %broadcast_compare_fusion, bf16[512,8,3,72]{0,3,2,1:T(8,128)(2,1)} %bitcast.211), kind=kOutput, calls=%fused_computation.234 | convolution fusion | flops 312476160 | bytes 10108928 | tf_op jit(solution)/shard_map/while/body/eval_jaxpr/sub | solution.py:208
  26.5 4.5 %fusion.67 = bf16[8,72,512]{2,1,0:T(8,128)(2,1)S(1)} fusion(f32[8,512,512]{1,2,0:T(8,128)} %get-tuple-element.51, f32[8,512]{1,0:T(8,128)S(1)} %get-tuple-element.50, bf16[512,8,3,72]{0,3,2,1:T(8,128)(2,1)} %bitcast.212), kind=kOutput, calls=%fused_computation.91 | convolution fusion | flops 306479104 | bytes 9584640 | tf_op jit(solution)/shard_map/while/body/eval_jaxpr/hqk,khd->qhd/dot_general | solution.py:210
  31.1 2.2 convolution_convert_fusion.1
  33.3 1.5 collective-permute-start
  34.8 26.3 %collective-permute-done.1 = bf16[1152,1024]{1,0:T(8,128)(2,1)} collective-permute-done((bf16[1152,1024]{1,0:T(8,128)(2,1)}, bf16[1152,1024]{1,0:T(8,128)(2,1)}, u32[]{:S(2)}, u32[]{:S(2)}) %collective-permute-start.1) | collective-permute-done | bytes 2359328 | tf_op jit(solution)/shard_map/ppermute | solution.py:25
  61.2 3.4 %fusion.10 = bf16[512,1152]{1,0:T(8,128)(2,1)} fusion(bf16[512,1152]{1,0:T(8,128)(2,1)} %param.10, bf16[512,1152]{1,0:T(8,128)(2,1)} %collective-permute-done, bf16[512,1152]{1,0:T(8,128)(2,1)} %convolution_convert_fusion.1), kind=kLoop, calls=%fused_computation.18 | loop fusion | flops 3538944 | bytes 4718592 | tf_op jit(solution)/shard_map/convert_element_type | solution.py:228
  64.6 2.6 convert_element_type.281
  67.3 2.4 fusion.134
  69.6 2.2 fusion.132
  71.9 2.2 fusion.130
  74.1 2.4 fusion.123
  77.4 83.7 %all-gather.3.cloned.1.call-done = bf16[4096,1152]{1,0:T(8,128)(2,1)} async-done(((bf16[128,1152]{1,0:T(8,128)(2,1)}), bf16[4096,1152]{1,0:T(8,128)(2,1)}) %all-gather.3.cloned.1.call-update) | async-done | bytes 9437200 | tf_op jit(solution)/shard_map/all_gather | solution.py:62
  161.2 4.6 %dynamic-slice_bitcast_fusion.1 = (bf16[4,2,128,1152]{3,2,1,0:T(8,128)(2,1)S(1)}, bf16[4,2,128,1152]{3,2,1,0:T(8,128)(2,1)S(1)}, bf16[4,2,128,1152]{3,2,1,0:T(8,128)(2,1)S(1)}, bf16[4,2,128,1152]{3,2,1,0:T(8,128)(2,1)S(1)}) fusion(bf16[4,4,2,128,1152]{4,3,2,1,0:T(8,128)(2,1)} %bitcast.173, s32[]{:T(128)S(6)} %select_n.94, s32[]{:T(128)S(6)} %select_n.96, ...), kind=kLoop, calls=%fused_computation.20 | loop fusion | bytes 18874384 | tf_op jit(solution)/shard_map/jit(dynamic_index_in_dim)/squeeze | solution.py:38
  165.8 1.9 fusion.164
  168.5 2.1 fusion.53
  170.6 2.2 fusion.51
  172.7 2.1 fusion.41
  174.8 2.1 fusion.39
  176.9 1.8 fusion.166
  179.4 2.1 fusion.49
  181.5 2.0 fusion.37
  184.2 2.1 fusion.47
  186.3 2.1 fusion.35
  190.1 1.6 slice.286
  191.6 1.0 copy.86
  197.0 3.2 %fusion.19 = f32[512,704]{0,1:T(8,128)S(1)} fusion(f32[512,704]{0,1:T(8,128)} %fusion.51, bf16[1,2048,704]{1,2,0:T(8,128)(2,1)} %param.17, bf16[512,1152]{1,0:T(8,128)(2,1)} %bitcast.188, f32[512]{0:T(512)S(1)} %bitcast.208), kind=kOutput, calls=%fused_computation.49 | convolution fusion | flops 738918400 | bytes 5376000 | tf_op jit(solution)/shard_map/dot_general | solution.py:86
  200.7 1.2 fusion.58
  202.7 1.0 fusion.143
  203.7 2.3 multiply_convert_fusion.4
  206.0 2.0 multiply_convert_fusion.6
  208.6 1.0 fusion.13
  210.0 1.2 fusion.64
  211.1 2.1 multiply_convert_fusion
  213.2 2.0 multiply_convert_fusion.2
  220.2 3.2 %fusion.22 = f32[512,704]{0,1:T(8,128)S(1)} fusion(f32[512,704]{0,1:T(8,128)} %fusion.53, bf16[1,2048,704]{1,2,0:T(8,128)(2,1)} %param.17, bf16[512,1152]{1,0:T(8,128)(2,1)} %bitcast.179, f32[512]{0:T(512)S(1)} %bitcast.202), kind=kOutput, calls=%fused_computation.54 | convolution fusion | flops 738918400 | bytes 5376000 | tf_op jit(solution)/shard_map/dot_general | solution.py:86
  223.9 1.0 fusion.16
  226.5 1.2 fusion.55
  227.9 1.2 fusion.61
  229.1 1.0 add_convert_fusion
  230.2 1.6 collective-permute-start.14
  231.7 2.2 add_convert_fusion.2
  235.3 1.5 collective-permute-start.9
  236.8 1.0 add_convert_fusion.1
  239.2 5.8 %collective-permute-done.14 = bf16[512,512]{1,0:T(8,128)(2,1)S(1)} collective-permute-done((bf16[512,512]{1,0:T(8,128)(2,1)S(1)}, bf16[512,512]{1,0:T(8,128)(2,1)S(1)}, u32[]{:S(2)}, u32[]{:S(2)}) %collective-permute-start.14) | collective-permute-done | bytes 524320 | tf_op jit(solution)/shard_map/ppermute | solution.py:25
  245.0 1.0 add_convert_fusion.5
  246.0 1.4 collective-permute-start.15
  247.4 13.6 %collective-permute-done.9 = bf16[512,512]{1,0:T(8,128)(2,1)S(1)} collective-permute-done((bf16[512,512]{1,0:T(8,128)(2,1)S(1)}, bf16[512,512]{1,0:T(8,128)(2,1)S(1)}, u32[]{:S(2)}, u32[]{:S(2)}) %collective-permute-start.9) | collective-permute-done | bytes 524320 | tf_op jit(solution)/shard_map/ppermute | solution.py:25
  261.0 1.0 add_convert_fusion.8
  262.6 2.4 add_convert_fusion.3
  265.0 6.4 %collective-permute-done.15 = bf16[512,512]{1,0:T(8,128)(2,1)} collective-permute-done((bf16[512,512]{1,0:T(8,128)(2,1)}, bf16[512,512]{1,0:T(8,128)(2,1)}, u32[]{:S(2)}, u32[]{:S(2)}) %collective-permute-start.15) | collective-permute-done | bytes 524320 | tf_op jit(solution)/shard_map/ppermute | solution.py:25
  271.4 2.9 collective-permute-done.10
  274.3 2.8 add_convert_fusion.7
  277.8 1.6 collective-permute-start.11
  279.4 1.0 dynamic-slice_bitcast_fusion.4
  281.0 6.6 %collective-permute-done.11 = bf16[2,128,512]{2,1,0:T(8,128)(2,1)} collective-permute-done((bf16[2,128,512]{2,1,0:T(8,128)(2,1)S(1)}, bf16[2,128,512]{2,1,0:T(8,128)(2,1)}, u32[]{:S(2)}, u32[]{:S(2)}) %collective-permute-start.11) | collective-permute-done | bytes 262176 | tf_op jit(solution)/shard_map/ppermute | solution.py:25
  287.6 1.1 fusion.126
  288.7 1.6 collective-permute-start.12
  290.4 1.3 collective-permute-done.16
  291.8 2.1 collective-permute-start.17
  293.9 2.2 collective-permute-done.12
  296.1 3.1 collective-permute-done.17
  (127 shorter events, 25.2 us)
Async XLA Ops:
  6.5 197.2 %copy-start = (bf16[1,704,2048]{2,1,0:T(8,128)(2,1)S(1)}, bf16[1,704,2048]{2,1,0:T(8,128)(2,1)}, u32[]{:S(2)}) copy-start(bf16[1,704,2048]{2,1,0:T(8,128)(2,1)} %param.19) | copy-start | bytes 8650756
  6.5 5.0 %copy-start.20 = (s32[1,4]{1,0:T(1,128)S(1)}, s32[1,4]{1,0:T(1,128)}, u32[]{:S(2)}) copy-start(s32[1,4]{1,0:T(1,128)} %param.11) | copy-start | bytes 52
  6.5 154.6 %all-gather.3.cloned.1.call-start = ((), (), s32[]{:S(2)}) async-start(), calls=%async_computation | async-start | bytes 9732096 | tf_op jit(solution)/shard_map/all_gather | solution.py:62
  6.5 4.5 %copy-start.1 = (bf16[512,1152]{1,0:T(8,128)(2,1)S(1)}, bf16[512,1152]{1,0:T(8,128)(2,1)}, u32[]{:S(2)}) copy-start(bf16[512,1152]{1,0:T(8,128)(2,1)} %param.10) | copy-start | bytes 3538948
  6.5 54.6 %collective-permute-start.1 = (bf16[1152,1024]{1,0:T(8,128)(2,1)}, bf16[1152,1024]{1,0:T(8,128)(2,1)}, u32[]{:S(2)}, u32[]{:S(2)}) collective-permute-start(bf16[1152,1024]{1,0:T(8,128)(2,1)} %param.14), channel_id=1, source_target_pairs={{0,8},{4,12},{8,0},{12,4},{1,9},{5,13},{9,1},{13,5},{2,10},{6,14},... | collective-permute-start | bytes 7077896 | tf_op jit(solution)/shard_map/ppermute | solution.py:25
  26.5 4.5 %copy-start.19 = (bf16[576,1152]{1,0:T(8,128)(2,1)S(1)}, bf16[576,1152]{1,0:T(8,128)(2,1)}, u32[]{:S(2)}) copy-start(bf16[576,1152]{1,0:T(8,128)(2,1)} %param.13) | copy-start | bytes 3981316
  31.1 30.1 %copy-start.11 = (f32[128,6]{0,1:T(8,128)S(1)}, f32[128,6]{0,1:T(8,128)}, u32[]{:S(2)}) copy-start(f32[128,6]{0,1:T(8,128)} %param.16) | copy-start | bytes 9220
  31.1 30.1 %copy-start.12 = (s32[128,6]{0,1:T(8,128)S(1)}, s32[128,6]{0,1:T(8,128)}, u32[]{:S(2)}) copy-start(s32[128,6]{0,1:T(8,128)} %param.15) | copy-start | bytes 9220
  33.3 27.9 %collective-permute-start = (bf16[512,1152]{1,0:T(8,128)(2,1)}, bf16[512,1152]{1,0:T(8,128)(2,1)}, u32[]{:S(2)}, u32[]{:S(2)}) collective-permute-start(bf16[512,1152]{1,0:T(8,128)(2,1)} %convolution_convert_fusion.1), channel_id=1, source_target_pairs={{0,16},{16,0},{1,17},{17,1},{2,18},{18,2},{3,19},{19,3},{4,20},{20... | collective-permute-start | bytes 3538952 | tf_op jit(solution)/shard_map/ppermute | solution.py:25
  34.8 37.1 %collective-permute-start.2 = (bf16[1152,1024]{1,0:T(8,128)(2,1)}, bf16[1152,1024]{1,0:T(8,128)(2,1)}, u32[]{:S(2)}, u32[]{:S(2)}) collective-permute-start(bf16[1152,1024]{1,0:T(8,128)(2,1)} %param.14), channel_id=1, source_target_pairs={{0,4},{4,0},{8,12},{12,8},{1,5},{5,1},{9,13},{13,9},{2,6},{6,2},{1... | collective-permute-start | bytes 7077896 | tf_op jit(solution)/shard_map/ppermute | solution.py:25
  61.1 12.9 %collective-permute-start.3 = (bf16[1152,1024]{1,0:T(8,128)(2,1)}, bf16[1152,1024]{1,0:T(8,128)(2,1)}, u32[]{:S(2)}, u32[]{:S(2)}) collective-permute-start(bf16[1152,1024]{1,0:T(8,128)(2,1)} %collective-permute-done.1), channel_id=1, source_target_pairs={{0,4},{4,0},{8,12},{12,8},{1,5},{5,1},{9,13},{13,9},{2,6},{6,2},{1... | collective-permute-start | bytes 7077896 | tf_op jit(solution)/shard_map/ppermute | solution.py:25
  67.3 2.4 copy-start.2
  165.8 2.7 copy-start.13
  170.5 2.2 copy-start.16
  188.5 4.9 %copy-start.9 = (bf16[512,128]{1,0:T(8,128)(2,1)S(1)}, bf16[512,128]{1,0:T(8,128)(2,1)}, u32[]{:S(2)}) copy-start(bf16[512,128]{1,0:T(8,128)(2,1)} %slice.297) | copy-start | bytes 393220
  189.3 4.9 %copy-start.10 = (bf16[512,128]{1,0:T(8,128)(2,1)S(1)}, bf16[512,128]{1,0:T(8,128)(2,1)}, u32[]{:S(2)}) copy-start(bf16[512,128]{1,0:T(8,128)(2,1)} %slice.309) | copy-start | bytes 393220
  197.0 3.3 %copy-start.8 = (bf16[4,1,128,1152]{3,2,1,0:T(8,128)(2,1)S(1)}, bf16[4,1,128,1152]{3,2,1,0:T(8,128)(2,1)}, u32[]{:S(2)}) copy-start(bf16[4,1,128,1152]{3,2,1,0:T(8,128)(2,1)} %get-tuple-element.55) | copy-start | bytes 3538948
  197.0 3.4 %copy-start.17 = (bf16[1,2048,704]{1,2,0:T(8,128)(2,1)S(1)}, bf16[1,2048,704]{1,2,0:T(8,128)(2,1)}, u32[]{:S(2)}) copy-start(bf16[1,2048,704]{1,2,0:T(8,128)(2,1)} %param.18) | copy-start | bytes 8650756
  197.0 3.8 %copy-start.26 = (f32[512,704]{0,1:T(8,128)S(1)}, f32[512,704]{0,1:T(8,128)}, u32[]{:S(2)}) copy-start(f32[512,704]{0,1:T(8,128)} %fusion.39) | copy-start | bytes 4325380
  203.7 4.3 %copy-start.22 = (f32[512,704]{0,1:T(8,128)S(1)}, f32[512,704]{0,1:T(8,128)}, u32[]{:S(2)}) copy-start(f32[512,704]{0,1:T(8,128)} %fusion.47) | copy-start | bytes 4325380
  206.0 2.0 copy-start.7
  206.0 2.6 copy-start.14
  208.6 1.4 copy-start.25
  217.1 14.6 %collective-permute-start.5 = (bf16[512,1024]{1,0:T(8,128)(2,1)}, bf16[512,1024]{1,0:T(8,128)(2,1)}, u32[]{:S(2)}, u32[]{:S(2)}) collective-permute-start(bf16[512,1024]{1,0:T(8,128)(2,1)} %multiply_convert_fusion.4), channel_id=1, source_target_pairs={{0,4},{4,0},{8,12},{12,8},{1,5},{5,1},{9,13},{13,9},{2,6},{6,2},{1... | collective-permute-start | bytes 3145736 | tf_op jit(solution)/shard_map/ppermute | solution.py:25
  219.3 9.7 %collective-permute-start.8 = (bf16[512,1024]{1,0:T(8,128)(2,1)}, bf16[512,1024]{1,0:T(8,128)(2,1)S(1)}, u32[]{:S(2)}, u32[]{:S(2)}) collective-permute-start(bf16[512,1024]{1,0:T(8,128)(2,1)} %multiply_convert_fusion), channel_id=1, source_target_pairs={{0,4},{4,0},{8,12},{12,8},{1,5},{5,1},{9,13},{13,9},{2,6},{6,2},{1... | collective-permute-start | bytes 3145736 | tf_op jit(solution)/shard_map/ppermute | solution.py:25
  219.6 42.9 %collective-permute-start.4 = (bf16[512,1024]{1,0:T(8,128)(2,1)}, bf16[512,1024]{1,0:T(8,128)(2,1)}, u32[]{:S(2)}, u32[]{:S(2)}) collective-permute-start(bf16[512,1024]{1,0:T(8,128)(2,1)} %multiply_convert_fusion.6), channel_id=1, source_target_pairs={{0,4},{4,0},{8,12},{12,8},{1,5},{5,1},{9,13},{13,9},{2,6},{6,2},{1... | collective-permute-start | bytes 3145736 | tf_op jit(solution)/shard_map/ppermute | solution.py:25
  219.9 16.9 %collective-permute-start.7 = (bf16[512,1024]{1,0:T(8,128)(2,1)}, bf16[512,1024]{1,0:T(8,128)(2,1)S(1)}, u32[]{:S(2)}, u32[]{:S(2)}) collective-permute-start(bf16[512,1024]{1,0:T(8,128)(2,1)} %multiply_convert_fusion.2), channel_id=1, source_target_pairs={{0,4},{4,0},{8,12},{12,8},{1,5},{5,1},{9,13},{13,9},{2,6},{6,2},{1... | collective-permute-start | bytes 3145736 | tf_op jit(solution)/shard_map/ppermute | solution.py:25
  220.1 3.2 %copy-start.6 = (bf16[4,1,128,1152]{3,2,1,0:T(8,128)(2,1)S(1)}, bf16[4,1,128,1152]{3,2,1,0:T(8,128)(2,1)}, u32[]{:S(2)}) copy-start(bf16[4,1,128,1152]{3,2,1,0:T(8,128)(2,1)} %get-tuple-element.38) | copy-start | bytes 3538948
  220.1 3.4 %copy-start.15 = (bf16[1,2048,704]{1,2,0:T(8,128)(2,1)S(1)}, bf16[1,2048,704]{1,2,0:T(8,128)(2,1)}, u32[]{:S(2)}) copy-start(bf16[1,2048,704]{1,2,0:T(8,128)(2,1)} %param.17) | copy-start | bytes 8650756
  220.2 3.8 %copy-start.21 = (f32[512,704]{0,1:T(8,128)S(1)}, f32[512,704]{0,1:T(8,128)}, u32[]{:S(2)}) copy-start(f32[512,704]{0,1:T(8,128)} %fusion.49) | copy-start | bytes 4325380
  223.9 1.3 copy-start.5
  223.9 2.2 copy-start.18
  223.9 2.6 copy-start.23
  226.5 1.4 copy-start.24
  227.9 3.9 %copy-start.27 = (bf16[512,704]{0,1:T(8,128)(2,1)}, bf16[512,704]{0,1:T(8,128)(2,1)S(1)}, u32[]{:S(2)}) copy-start(bf16[512,704]{0,1:T(8,128)(2,1)S(1)} %fusion.55) | copy-start | bytes 2162692
  230.2 14.8 %collective-permute-start.14 = (bf16[512,512]{1,0:T(8,128)(2,1)S(1)}, bf16[512,512]{1,0:T(8,128)(2,1)S(1)}, u32[]{:S(2)}, u32[]{:S(2)}) collective-permute-start(bf16[512,512]{1,0:T(8,128)(2,1)S(1)} %get-tuple-element.45), channel_id=1, source_target_pairs={{0,8},{4,12},{8,0},{12,4},{1,9},{5,13},{9,1},{13,5},{2,10},{6,14},... | collective-permute-start | bytes 1572872 | tf_op jit(solution)/shard_map/ppermute | solution.py:25
  234.8 30.2 %collective-permute-start.6 = (bf16[512,512]{1,0:T(8,128)(2,1)}, bf16[512,512]{1,0:T(8,128)(2,1)}, u32[]{:S(2)}, u32[]{:S(2)}) collective-permute-start(bf16[512,512]{1,0:T(8,128)(2,1)} %slice.292), channel_id=1, source_target_pairs={{0,16},{16,0},{1,17},{17,1},{2,18},{18,2},{3,19},{19,3},{4,20},{20... | collective-permute-start | bytes 1572872 | tf_op jit(solution)/shard_map/ppermute | solution.py:25
  235.3 25.7 %collective-permute-start.9 = (bf16[512,512]{1,0:T(8,128)(2,1)S(1)}, bf16[512,512]{1,0:T(8,128)(2,1)S(1)}, u32[]{:S(2)}, u32[]{:S(2)}) collective-permute-start(bf16[512,512]{1,0:T(8,128)(2,1)S(1)} %get-tuple-element.44), channel_id=1, source_target_pairs={{0,16},{16,0},{1,17},{17,1},{2,18},{18,2},{3,19},{19,3},{4,20},{20... | collective-permute-start | bytes 1572872 | tf_op jit(solution)/shard_map/ppermute | solution.py:25
  238.7 26.3 %collective-permute-start.13 = (bf16[512,512]{1,0:T(8,128)(2,1)}, bf16[512,512]{1,0:T(8,128)(2,1)}, u32[]{:S(2)}, u32[]{:S(2)}) collective-permute-start(bf16[512,512]{1,0:T(8,128)(2,1)} %slice.320), channel_id=1, source_target_pairs={{0,8},{4,12},{8,0},{12,4},{1,9},{5,13},{9,1},{13,5},{2,10},{6,14},... | collective-permute-start | bytes 1572872 | tf_op jit(solution)/shard_map/ppermute | solution.py:25
  246.0 25.4 %collective-permute-start.15 = (bf16[512,512]{1,0:T(8,128)(2,1)}, bf16[512,512]{1,0:T(8,128)(2,1)}, u32[]{:S(2)}, u32[]{:S(2)}) collective-permute-start(bf16[512,512]{1,0:T(8,128)(2,1)} %add_convert_fusion.5), channel_id=1, source_target_pairs={{0,16},{16,0},{1,17},{17,1},{2,18},{18,2},{3,19},{19,3},{4,20},{20... | collective-permute-start | bytes 1572872 | tf_op jit(solution)/shard_map/ppermute | solution.py:25
  262.0 12.3 %collective-permute-start.10 = (bf16[512,512]{1,0:T(8,128)(2,1)}, bf16[512,512]{1,0:T(8,128)(2,1)}, u32[]{:S(2)}, u32[]{:S(2)}) collective-permute-start(bf16[512,512]{1,0:T(8,128)(2,1)} %add_convert_fusion.8), channel_id=1, source_target_pairs={{0,8},{4,12},{8,0},{12,4},{1,9},{5,13},{9,1},{13,5},{2,10},{6,14},... | collective-permute-start | bytes 1572872 | tf_op jit(solution)/shard_map/ppermute | solution.py:25
  277.0 0.8 copy-start.4
  277.8 9.8 %collective-permute-start.11 = (bf16[2,128,512]{2,1,0:T(8,128)(2,1)S(1)}, bf16[2,128,512]{2,1,0:T(8,128)(2,1)}, u32[]{:S(2)}, u32[]{:S(2)}) collective-permute-start(bf16[2,128,512]{2,1,0:T(8,128)(2,1)S(1)} %dynamic-slice_bitcast_fusion.5), channel_id=1, source_target_pairs={{0,1},{1,0},{2,3},{3,2},{4,5},{5,4},{6,7},{7,6},{8,9},{9,8},{10,11... | collective-permute-start | bytes 786440 | tf_op jit(solution)/shard_map/ppermute | solution.py:25
  279.4 12.3 %copy-start.3 = (bf16[512,512]{1,0:T(8,128)(2,1)S(1)}, bf16[512,512]{1,0:T(8,128)(2,1)}, u32[]{:S(2)}) copy-start(bf16[512,512]{1,0:T(8,128)(2,1)} %get-tuple-element.43) | copy-start | bytes 1572868
  280.4 11.3 %collective-permute-start.16 = (bf16[2,128,512]{2,1,0:T(8,128)(2,1)S(1)}, bf16[2,128,512]{2,1,0:T(8,128)(2,1)S(1)}, u32[]{:S(2)}, u32[]{:S(2)}) collective-permute-start(bf16[2,128,512]{2,1,0:T(8,128)(2,1)S(1)} %dynamic-slice_bitcast_fusion.4), channel_id=1, source_target_pairs={{0,1},{1,0},{2,3},{3,2},{4,5},{5,4},{6,7},{7,6},{8,9},{9,8},{10,11... | collective-permute-start | bytes 786440 | tf_op jit(solution)/shard_map/ppermute | solution.py:25
  288.7 7.3 %collective-permute-start.12 = (bf16[128,512]{1,0:T(8,128)(2,1)S(1)}, bf16[128,512]{1,0:T(8,128)(2,1)S(1)}, u32[]{:S(2)}, u32[]{:S(2)}) collective-permute-start(bf16[128,512]{1,0:T(8,128)(2,1)S(1)} %dynamic-slice_bitcast_fusion.7), channel_id=1, source_target_pairs={{0,2},{1,3},{2,0},{3,1},{4,6},{5,7},{6,4},{7,5},{8,10},{9,11},{10,... | collective-permute-start | bytes 393224 | tf_op jit(solution)/shard_map/ppermute | solution.py:25
  291.8 7.3 %collective-permute-start.17 = (bf16[128,512]{1,0:T(8,128)(2,1)S(1)}, bf16[128,512]{1,0:T(8,128)(2,1)S(1)}, u32[]{:S(2)}, u32[]{:S(2)}) collective-permute-start(bf16[128,512]{1,0:T(8,128)(2,1)S(1)} %dynamic-slice_bitcast_fusion.6), channel_id=1, source_target_pairs={{0,2},{1,3},{2,0},{3,1},{4,6},{5,7},{6,4},{7,5},{8,10},{9,11},{10,... | collective-permute-start | bytes 393224 | tf_op jit(solution)/shard_map/ppermute | solution.py:25
Sparse Core Ops, SparseCore 0:
  77.5 83.6 all-gather.2

commit v3 on v2

--- a/solution.py
+++ b/solution.py
@@ -25,89 +25,95 @@
     return lax.ppermute(values, axis, [(i, i ^ bit) for i in range(count)])
 
 
-def halves(values):
-    high = lax.reduce_precision(values, 8, 7)
-    return [high.astype(jnp.bfloat16), (values - high).astype(jnp.bfloat16)]
-
-
 def pair_sum(own, other):
     return (own.astype(jnp.float32) + other.astype(jnp.float32)).astype(jnp.bfloat16)
 
 
-def pick(values, index, axis):
-    return lax.dynamic_index_in_dim(values, index, axis, keepdims=False)
-
-
-def dense_experts(proj_own, routes, gates, w_gate, w_up, w_down):
+def along_expert(values):
+    far = jnp.stack([values, swapped(values, "expert", 2)])
+    return jnp.concatenate([far, swapped(far, "expert", 1)])
+
+
+def expert_weights(routes, gates):
+    owners = lax.axis_size("expert")
+    groups = lax.axis_size("dp") * owners
+    own_expert = lax.axis_index("dp") * owners + lax.axis_index("expert")
+    at_expert = jnp.arange(groups, dtype=jnp.int32)[None, :]
+    per_expert = jnp.sum(
+        jnp.where(routes[:, :, None] == at_expert[None], gates[:, :, None], 0.0), axis=1
+    )
+    found = {0: along_expert(per_expert)}
+    found[2] = swapped(found[0], "dp", 2)
+    for flip in (0, 2):
+        found[flip + 1] = swapped(found[flip], "dp", 1)
+    return {
+        flip: jnp.sum(
+            jnp.where(at_expert == own_expert, piece.reshape(-1, groups), 0.0),
+            axis=1,
+            keepdims=True,
+        )
+        for flip, piece in found.items()
+    }
+
+
+def dense_experts(proj_own, weights, w_gate, w_up, w_down):
     sections = lax.axis_size("section")
     data_count = lax.axis_size("dp")
     owners = lax.axis_size("expert")
-    groups = data_count * owners
     rows, part = proj_own.shape
-    me_d, me_e, me_s = lax.axis_index("dp"), lax.axis_index("expert"), lax.axis_index("section")
-    per_expert = jnp.sum(
-        jnp.where(
-            routes[:, :, None] == jnp.arange(groups, dtype=jnp.int32)[None, None, :],
-            gates[:, :, None],
-            0.0,
-        ),
-        axis=1,
-    )
+    me_s = lax.axis_index("section")
     own = proj_own.astype(jnp.float32)
-    side = halves(per_expert) + halves(jnp.sum(own * own, axis=1, keepdims=True))
-    side = jnp.concatenate(side, axis=1)
-    side_width = -(-side.shape[1] // 128) * 128
-    side = jnp.pad(side, ((0, 0), (0, side_width - side.shape[1])))
-    sent = jnp.concatenate([proj_own, side], axis=1)
-    gathered = lax.all_gather(sent, ("dp", "expert", "section"), axis=0, tiled=False)
-    gathered = gathered.reshape(data_count, owners, sections, rows, part + side_width)
+    squares = jnp.sum(own * own, axis=1)
+    squares = squares + swapped(squares, "section", 1)
+    normed = (own * lax.rsqrt(squares / (sections * part) + 1e-06)[:, None]).astype(jnp.bfloat16)
+    half = part // 2
+    left = {(0, 0): along_expert(normed[:, :half]).reshape(owners * rows, half)}
+    right = {(0, 0): along_expert(normed[:, half:]).reshape(owners * rows, half)}
+    left[0, 1] = swapped(left[0, 0], "section", 1)
+    right[2, 0] = swapped(right[0, 0], "dp", 2)
+    right[0, 1] = swapped(right[0, 0], "section", 1)
+    left[2, 0] = swapped(left[0, 0], "dp", 2)
+    left[2, 1] = swapped(left[0, 1], "dp", 2)
+    right[2, 1] = swapped(right[2, 0], "section", 1)
+    tokens = {}
+    for flip in (0, 2):
+        pieces = [side[flip, q] for q in range(sections) for side in (left, right)]
+        tokens[flip] = jnp.concatenate(pieces, axis=1)
+        tokens[flip + 1] = jnp.concatenate([swapped(p, "dp", 1) for p in pieces], axis=1)
+
+    def turned(matrix):
+        return jnp.concatenate(
+            [
+                lax.dynamic_slice_in_dim(matrix[0], (me_s ^ flip) * part, part, axis=0)
+                for flip in range(sections)
+            ],
+            axis=0,
+        )
+
+    w_gate, w_up = turned(w_gate), turned(w_up)
     down = [
         lax.dynamic_slice_in_dim(w_down[0], (me_s ^ flip) * part, part, axis=1)
         for flip in range(sections)
     ]
-    own_expert = me_d * owners + me_e
-    at_expert = jnp.arange(groups, dtype=jnp.int32)[None, :] == own_expert
-
-    def run(flip_d):
-        block = pick(gathered, me_d ^ flip_d, 0)
-        block = [block[:, q].reshape(owners * rows, part + side_width) for q in range(sections)]
-        tokens = [piece[:, :part] for piece in block]
-        sides = [piece[:, part:].astype(jnp.float32) for piece in block]
-        weight = sides[0][:, :groups] + sides[0][:, groups : 2 * groups]
-        weight = jnp.sum(jnp.where(at_expert, weight, 0.0), axis=1, keepdims=True)
-        squares = sum(
-            piece[:, 2 * groups : 2 * groups + 1] + piece[:, 2 * groups + 1 : 2 * groups + 2]
-            for piece in sides
-        )
-        inverse = lax.rsqrt(squares / (sections * part) + 1e-06)
-
-        def through(matrix):
-            product = sum(
-                jnp.dot(
-                    piece,
-                    matrix[0, q * part : (q + 1) * part],
-                    preferred_element_type=jnp.float32,
-                )
-                for q, piece in enumerate(tokens)
-            )
-            return product * inverse
-
-        hidden = (jax.nn.silu(through(w_gate)) * through(w_up)).astype(jnp.bfloat16)
+
+    def run(flip):
+        gate_act = jnp.dot(tokens[flip], w_gate, preferred_element_type=jnp.float32)
+        up_act = jnp.dot(tokens[flip], w_up, preferred_element_type=jnp.float32)
+        hidden = (jax.nn.silu(gate_act) * up_act).astype(jnp.bfloat16)
         return [
-            (jnp.dot(hidden, piece, preferred_element_type=jnp.float32) * weight).astype(
+            (jnp.dot(hidden, piece, preferred_element_type=jnp.float32) * weights[flip]).astype(
                 jnp.bfloat16
             )
             for piece in down
         ]
 
-    partial = {flip: run(flip) for flip in sorted(range(data_count), key=lambda f: (-(f & 1), -f))}
+    partial = {flip: run(flip) for flip in range(data_count)}
     near = {}
     for flip in range(data_count - 2, -1, -2):
         near[flip] = [
             pair_sum(partial[flip][q], swapped(partial[flip + 1][q], "dp", 1))
             for q in range(sections)
         ]
-    half = part // 2
     left = [piece[:, :half] for piece in near[0]], [piece[:, :half] for piece in near[2]]
     right = [piece[:, half:] for piece in near[0]], [piece[:, half:] for piece in near[2]]
     far_left = pair_sum(left[1][0], swapped(left[1][1], "section", 1))
@@ -118,13 +124,10 @@
     mid_right = pair_sum(mid_right, swapped(far_right, "section", 1))
     ends = []
     for piece in (mid_left, mid_right):
-        piece = piece.reshape(owners // 2, 2, rows, half)
-        low = me_e & 1
-        piece = pair_sum(pick(piece, low, 1), swapped(pick(piece, 1 - low, 1), "expert", 1))
-        high = me_e // 2
+        piece = piece.reshape(owners, rows, half)
+        piece = pair_sum(piece[:2], swapped(piece[2:], "expert", 1))
         ends.append(
-            pick(piece, high, 0).astype(jnp.float32)
-            + swapped(pick(piece, 1 - high, 0), "expert", 2).astype(jnp.float32)
+            piece[0].astype(jnp.float32) + swapped(piece[1], "expert", 2).astype(jnp.float32)
         )
     return (own + jnp.concatenate(ends, axis=1)).astype(jnp.bfloat16)
 
@@ -179,6 +182,12 @@
     head_dim = D_VIT // HEADS
     local_heads = w_qkv.shape[1] // (3 * head_dim)
     scale = 1.0 / math.sqrt(head_dim)
+    merged_count = patch_rows // 4
+    expert_total = data_count * owner_count
+    capacity = max(2, min(merged_count, 2 * merged_count * TOP // expert_total))
+    shape = (lax.axis_size("section"), data_count, owner_count)
+    dense = shape == (2, 4, 4) and merged_count <= 2 * capacity
+    weights = expert_weights(routes, gates) if dense else None
     shards = [(0, w_proj)]
     bit = data_count // 2
     while bit >= 1:
@@ -218,7 +227,6 @@
         ),
     )
     attended = attended.reshape(patch_rows, local_heads * head_dim)
-    merged_count = patch_rows // 4
     mixed = jnp.dot(attended, w_out, preferred_element_type=jnp.float32).astype(jnp.bfloat16)
     if lax.axis_size("section") == 2:
         summed = mixed.astype(jnp.float32) + swapped(mixed, "section", 1).astype(jnp.float32)
@@ -237,11 +245,8 @@
         )
         for flip, shard in shards
     ).astype(jnp.bfloat16)
-    expert_total = data_count * owner_count
-    capacity = max(2, min(merged_count, 2 * merged_count * TOP // expert_total))
-    shape = (lax.axis_size("section"), data_count, owner_count)
-    if shape == (2, 4, 4) and merged_count <= 2 * capacity:
-        return dense_experts(proj_own, routes, gates, w_gate, w_up, w_down)
+    if dense:
+        return dense_experts(proj_own, weights, w_gate, w_up, w_down)
     return routed_experts(proj_own, routes, gates, w_gate, w_up, w_down, capacity)
 
 

time: 308 us -> 232 us (0.75)
  waiting for transfers between devices: 152 us -> 108 us
  starting transfers between devices: 17.6 us -> 39.4 us
  matrix products: 75.1 us -> 57.2 us
  local copies, waits for them, and re-layouts: 26.8 us -> 11 us
  between operations: 14 us -> 0.6 us
  other arithmetic: 21.3 us -> 15 us
    all_gather x1 -> x0, waiting for transfers between devices: 83.7 us -> none  [dense_experts(): lax.all_gather(sent, ('dp', 'expert', 'section'), axis=0, tiled=False)]
    ppermute x18 -> x42, waiting for transfers between devices: 68.2 us -> 108 us  [swapped(): return lax.ppermute(values, axis, [(i, i ^ bit) for i in range(count)])]
    ppermute x18 -> x42, starting transfers between devices: 17.6 us -> 39.4 us  [swapped(): return lax.ppermute(values, axis, [(i, i ^ bit) for i in range(count)])]
    dot_general x24 -> x16, matrix products: 44.8 us -> 26.8 us  [the longest x4 9.78 us: run(): gate_act = jnp.dot(tokens[flip], w_gate, preferred_element_type=jnp.float32)]
    slice x10 -> x2, local copies, waits for them, and re-layouts: 9.4 us -> 0.07 us  [dense_experts(): piece = pair_sum(piece[:2], swapped(piece[2:], 'expert', 1))]
    squeeze x5 -> x2, local copies, waits for them, and re-layouts: 5.72 us -> 0.02 us  [dense_experts(): piece[1]]
    dynamic_slice x0 -> x1, local copies, waits for them, and re-layouts: none -> 5.25 us  [turned(): lax.dynamic_slice_in_dim(matrix[0], (me_s ^ flip) * part, part, axis=0)]
    convert_element_type x5, other arithmetic: 5.87 us -> 0.94 us  [pair_sum(): (own.astype(jnp.float32) + other.astype(jnp.float32)).astype(jnp.bfloat16)]
  transfers between devices with their start and end apart: 19 -> 42, of which waited for: 10 -> 20; matrix products, arithmetic and copies ran while one was open for 19% -> 33% of each run, Pallas kernels for 0% -> 0%
where the time goes in v3:
time: 232 us; the launch traced here: 231 us
  waiting for transfers between devices  108 us (47%)
  matrix products  57.2 us (25%)
  starting transfers between devices  39.4 us (17%)
  other arithmetic  15 us (6%)
  local copies, waits for them, and re-layouts  11 us (5%)
    ppermute x42, waiting for transfers between devices, swapped(): return lax.ppermute(values, axis, [(i, i ^ bit) for i in range(count)])  108 us
    ppermute x42, starting transfers between devices, swapped(): return lax.ppermute(values, axis, [(i, i ^ bit) for i in range(count)])  39.4 us
    dot_general x4, matrix products, run(): gate_act = jnp.dot(tokens[flip], w_gate, preferred_element_type=jnp.float32)  9.78 us
    dot_general x4, matrix products, per_device(): jnp.dot(lax.dynamic_slice_in_dim(merged, (me_d ^ flip) * depth, depth, ax...  9.14 us
    dot_general x4, matrix products, run(): up_act = jnp.dot(tokens[flip], w_up, preferred_element_type=jnp.float32)  8.89 us
    dot_general x8, matrix products, run(): jnp.dot(hidden, piece, preferred_element_type=jnp.float32) * weights[flip]  8.16 us
    sub x1, matrix products, attend(): weights = jnp.where(same[None], jnp.exp(scores - peak), 0.0)  8.09 us
    dot_general x1, matrix products, per_device(): jnp.dot(normed_in, w_qkv, preferred_element_type=jnp.float32)  6.39 us
  transfers between devices with their start and end apart: 42, of which 20 were waited for; matrix products, arithmetic and copies ran while one was open for 33% of the time, Pallas kernels for 0%

profile of v3, /device:TPU:0, one launch (start us, length us, event | category | flops | bytes accessed | tf_op | source)
XLA Modules:
  0.0 231.2 jit_solution(4546691241127076931)
XLA Ops:
  0.0 3.0 %collective-permute-start.1 = (bf16[1152,1024]{1,0:T(8,128)(2,1)}, bf16[1152,1024]{1,0:T(8,128)(2,1)}, u32[]{:S(2)}, u32[]{:S(2)}) collective-permute-start(bf16[1152,1024]{1,0:T(8,128)(2,1)} %param.14), channel_id=1, source_target_pairs={{0,8},{4,12},{8,0},{12,4},{1,9},{5,13},{9,1},{13,5},{2,10},{6,14},... | collective-permute-start | bytes 7077896 | tf_op jit(solution)/shard_map/ppermute | solution.py:25
  3.0 1.5 convert_reduce_fusion
  4.5 1.7 fusion.8
  6.7 6.4 %convolution_convert_fusion = bf16[512,1728]{0,1:T(8,128)(2,1)} fusion(bf16[1152,1728]{0,1:T(8,128)(2,1)} %param.12, bf16[512,1152]{1,0:T(8,128)(2,1)} %param.10, f32[512]{0:T(512)S(1)} %add_rsqrt_fusion, f32[512]{0:T(512)S(1)} %broadcast_multiply_fusion), kind=kOutput, calls=%fused_computation.12 | convolution fusion | flops 2041675776 | bytes 6934528 | tf_op jit(solution)/shard_map/dot_general | solution.py:197
  13.1 8.1 %fusion.81 = (f32[8,512]{1,0:T(8,128)S(1)}, f32[8,512,512]{1,2,0:T(8,128)}) fusion(pred[512,512]{0,1:T(8,128)(4,1)S(1)} %broadcast_compare_fusion, bf16[512,8,3,72]{0,3,2,1:T(8,128)(2,1)} %bitcast.150), kind=kOutput, calls=%fused_computation.157 | convolution fusion | flops 312476160 | bytes 10108928 | tf_op jit(solution)/shard_map/while/body/eval_jaxpr/sub | solution.py:217
  21.2 4.5 %fusion.19 = bf16[8,72,512]{2,1,0:T(8,128)(2,1)S(1)} fusion(f32[8,512,512]{1,2,0:T(8,128)} %get-tuple-element.47, f32[8,512]{1,0:T(8,128)S(1)} %get-tuple-element.46, bf16[512,8,3,72]{0,3,2,1:T(8,128)(2,1)} %bitcast.151), kind=kOutput, calls=%fused_computation.50 | convolution fusion | flops 306479104 | bytes 9584640 | tf_op jit(solution)/shard_map/while/body/eval_jaxpr/hqk,khd->qhd/dot_general | solution.py:219
  25.7 2.3 convolution_convert_fusion.1
  28.0 1.5 collective-permute-start
  29.5 25.1 %collective-permute-done.1 = bf16[1152,1024]{1,0:T(8,128)(2,1)} collective-permute-done((bf16[1152,1024]{1,0:T(8,128)(2,1)}, bf16[1152,1024]{1,0:T(8,128)(2,1)}, u32[]{:S(2)}, u32[]{:S(2)}) %collective-permute-start.1) | collective-permute-done | bytes 2359328 | tf_op jit(solution)/shard_map/ppermute | solution.py:25
  54.5 1.2 collective-permute-done
  55.7 3.5 %fusion.10 = bf16[512,1152]{1,0:T(8,128)(2,1)} fusion(bf16[512,1152]{1,0:T(8,128)(2,1)} %param.10, bf16[512,1152]{1,0:T(8,128)(2,1)} %collective-permute-done, bf16[512,1152]{1,0:T(8,128)(2,1)} %convolution_convert_fusion.1), kind=kLoop, calls=%fused_computation.20 | loop fusion | flops 3538944 | bytes 4718592 | tf_op jit(solution)/shard_map/convert_element_type | solution.py:236
  59.2 2.6 %convert_element_type.230 = bf16[128,4608]{1,0:T(8,128)(2,1)} reshape(bf16[512,1152]{1,0:T(8,128)(2,1)} %fusion.10) | data formatting | bytes 2359296 | tf_op jit(solution)/shard_map/convert_element_type | solution.py:236
  61.8 2.4 %fusion.54 = f32[128,1024]{1,0:T(8,128)S(1)} fusion(bf16[1152,1024]{1,0:T(8,128)(2,1)} %param.14, bf16[128,4608]{1,0:T(8,128)(2,1)} %convert_element_type.230, s32[]{:T(128)S(6)} %select_n.54), kind=kOutput, calls=%fused_computation.93 | convolution fusion | flops 301989888 | bytes 3178500 | tf_op jit(solution)/shard_map/dot_general | solution.py:241
  64.2 2.2 fusion.52
  66.4 2.2 fusion.50
  68.6 2.4 %multiply_reduce_fusion = (f32[128]{0:T(128)S(1)}, f32[128,1024]{1,0:T(8,128)S(1)}) fusion(bf16[1152,1024]{1,0:T(8,128)(2,1)} %collective-permute-done.3, bf16[128,4608]{1,0:T(8,128)(2,1)S(1)} %copy-done.1, s32[]{:T(128)S(6)} %select_n.57, f32[128,1024]{1,0:T(8,128)S(1)} %fusion.50, f32[128,1024]{1,0:T(8,128)S(1)} %fusion.54, f32[128,1024]{1,0:T(8,128)S(1)} %fusion.52), kind=kOutput, calls=%fused_computation.83 | convolution fusion | flops 302907264 | bytes 4751876 | tf_op jit(solution)/shard_map/dot_general | solution.py:241
  71.0 1.6 collective-permute-start.4
  72.6 2.0 collective-permute-done.4
  74.8 2.7 %collective-permute-start.7 = (bf16[128,512]{1,0:T(8,128)(2,1)S(1)}, bf16[128,512]{1,0:T(8,128)(2,1)S(1)}, u32[]{:S(2)}, u32[]{:S(2)}) collective-permute-start(bf16[128,512]{1,0:T(8,128)(2,1)S(1)} %get-tuple-element.44), channel_id=1, source_target_pairs={{0,2},{1,3},{2,0},{3,1},{4,6},{5,7},{6,4},{7,5},{8,10},{9,11},{10,... | collective-permute-start | bytes 393224 | tf_op jit(solution)/shard_map/ppermute | solution.py:25
  77.8 8.6 %collective-permute-done.7 = bf16[128,512]{1,0:T(8,128)(2,1)S(1)} collective-permute-done((bf16[128,512]{1,0:T(8,128)(2,1)S(1)}, bf16[128,512]{1,0:T(8,128)(2,1)S(1)}, u32[]{:S(2)}, u32[]{:S(2)}) %collective-permute-start.7) | collective-permute-done | bytes 131104 | tf_op jit(solution)/shard_map/ppermute | solution.py:25
  89.3 1.3 collective-permute-start.6
  90.6 2.9 %collective-permute-start.11 = (f32[128,16]{0,1:T(8,128)S(1)}, f32[128,16]{0,1:T(8,128)S(1)}, u32[]{:S(2)}, u32[]{:S(2)}) collective-permute-start(f32[128,16]{0,1:T(8,128)S(1)} %select_reduce_fusion), channel_id=1, source_target_pairs={{0,2},{1,3},{2,0},{3,1},{4,6},{5,7},{6,4},{7,5},{8,10},{9,11},{10,... | collective-permute-start | bytes 24584 | tf_op jit(solution)/shard_map/ppermute | solution.py:25
  93.5 4.9 %collective-permute-done.11 = f32[128,16]{0,1:T(8,128)S(1)} collective-permute-done((f32[128,16]{0,1:T(8,128)S(1)}, f32[128,16]{0,1:T(8,128)S(1)}, u32[]{:S(2)}, u32[]{:S(2)}) %collective-permute-start.11) | collective-permute-done | bytes 8224 | tf_op jit(solution)/shard_map/ppermute | solution.py:25
  98.3 4.1 %collective-permute-start.12 = (f32[2,128,16]{1,2,0:T(8,128)S(1)}, f32[2,128,16]{1,2,0:T(8,128)S(1)}, u32[]{:S(2)}, u32[]{:S(2)}) collective-permute-start(f32[2,128,16]{1,2,0:T(8,128)S(1)} %pad_maximum_fusion.12), channel_id=1, source_target_pairs={{0,1},{1,0},{2,3},{3,2},{4,5},{5,4},{6,7},{7,6},{8,9},{9,8},{10,11... | collective-permute-start | bytes 49160 | tf_op jit(solution)/shard_map/ppermute | solution.py:25
  102.4 1.9 pad_maximum_fusion.4
  104.3 1.5 collective-permute-start.10
  105.8 1.9 pad_maximum_fusion.3
  109.5 1.5 collective-permute-start.25
  111.0 5.2 %dynamic-slice_bitcast_fusion.1 = (bf16[1024,704]{0,1:T(8,128)(2,1)}, bf16[1024,704]{0,1:T(8,128)(2,1)}, bf16[1024,704]{0,1:T(8,128)(2,1)}, bf16[1024,704]{0,1:T(8,128)(2,1)}) fusion(bf16[1,2048,704]{1,2,0:T(8,128)(2,1)} %param.18, s32[]{:T(128)S(6)} %select_n.58, s32[]{:T(128)S(6)} %select_n.59, bf16[1,2048,704]{1,2,0:T(8,128)(2,1)} %param.17), kind=kLoop, calls=%fused_computation.47 | loop fusion | bytes 11534344 | tf_op jit(solution)/shard_map/dynamic_slice | solution.py:87
  119.5 1.5 collective-permute-start.21
  121.0 7.5 %collective-permute-done.9 = bf16[512,512]{1,0:T(8,128)(2,1)} collective-permute-done((bf16[512,512]{1,0:T(8,128)(2,1)}, bf16[512,512]{1,0:T(8,128)(2,1)}, u32[]{:S(2)}, u32[]{:S(2)}) %collective-permute-start.9) | collective-permute-done | bytes 524320 | tf_op jit(solution)/shard_map/ppermute | solution.py:25
  128.5 4.3 %fusion.48 = f32[512,704]{0,1:T(8,128)S(1)} fusion(bf16[512,512]{1,0:T(8,128)(2,1)} %collective-permute-done.10, bf16[512,512]{1,0:T(8,128)(2,1)} %collective-permute-done.9, bf16[512,512]{1,0:T(8,128)(2,1)} %bitcast.13, bf16[512,512]{1,0:T(8,128)(2,1)} %bitcast.10, bf16[1024,704]{0,1:T(8,128)(2,1)} %get-tuple-element.50, ...), kind=kOutput, calls=%fused_computation.87 | convolution fusion | flops 1490550784 | bytes 6422528 | tf_op jit(solution)/shard_map/dot_general | solution.py:100
  132.8 3.4 %multiply_convert_fusion.11 = bf16[512,704]{0,1:T(8,128)(2,1)S(1)} fusion(f32[512,704]{0,1:T(8,128)S(1)} %fusion.48, bf16[512,512]{1,0:T(8,128)(2,1)} %collective-permute-done.10, bf16[512,512]{1,0:T(8,128)(2,1)} %collective-permute-done.9, bf16[512,512]{1,0:T(8,128)(2,1)} %bitcast.13, bf16[512,512]{1,0:T(8,128)(2,1)} %bitcast.10, ...), kind=kOutput, calls=%fused_computation.45 | convolution fusion | flops 1492713472 | bytes 7143424 | tf_op jit(solution)/shard_map/dot_general | solution.py:101
  136.9 1.6 collective-permute-start.23
  138.4 6.1 %collective-permute-done.21 = bf16[512,512]{1,0:T(8,128)(2,1)S(1)} collective-permute-done((bf16[512,512]{1,0:T(8,128)(2,1)}, bf16[512,512]{1,0:T(8,128)(2,1)S(1)}, u32[]{:S(2)}, u32[]{:S(2)}) %collective-permute-start.21) | collective-permute-done | bytes 524320 | tf_op jit(solution)/shard_map/ppermute | solution.py:25
  144.5 1.5 collective-permute-start.24
  147.9 1.8 fusion.77
  149.6 1.8 multiply_convert_fusion.10
  151.5 1.0 multiply_convert_fusion.4
  152.6 2.5 %collective-permute-done.23 = bf16[512,512]{1,0:T(8,128)(2,1)S(1)} collective-permute-done((bf16[512,512]{1,0:T(8,128)(2,1)}, bf16[512,512]{1,0:T(8,128)(2,1)S(1)}, u32[]{:S(2)}, u32[]{:S(2)}) %collective-permute-start.23) | collective-permute-done | bytes 524320 | tf_op jit(solution)/shard_map/ppermute | solution.py:25
  155.1 2.1 collective-permute-done.24
  157.5 2.0 fusion.76
  159.7 1.8 fusion.75
  161.4 1.8 multiply_convert_fusion.8
  163.3 1.0 multiply_convert_fusion
  164.9 1.8 multiply_convert_fusion.9
  167.8 1.0 multiply_convert_fusion.6
  169.4 1.0 add_convert_fusion
  171.1 1.0 add_convert_fusion.2
  172.2 1.6 collective-permute-start.20
  174.3 1.0 add_convert_fusion.1
  175.3 1.6 collective-permute-start.37
  176.9 8.4 %collective-permute-done.38 = bf16[512,512]{1,0:T(8,128)(2,1)S(1)} collective-permute-done((bf16[512,512]{1,0:T(8,128)(2,1)S(1)}, bf16[512,512]{1,0:T(8,128)(2,1)S(1)}, u32[]{:S(2)}, u32[]{:S(2)}) %collective-permute-start.38) | collective-permute-done | bytes 524320 | tf_op jit(solution)/shard_map/ppermute | solution.py:25
  185.5 1.5 collective-permute-start.39
  187.1 11.2 %collective-permute-done.33 = bf16[512,512]{1,0:T(8,128)(2,1)S(1)} collective-permute-done((bf16[512,512]{1,0:T(8,128)(2,1)S(1)}, bf16[512,512]{1,0:T(8,128)(2,1)S(1)}, u32[]{:S(2)}, u32[]{:S(2)}) %collective-permute-start.33) | collective-permute-done | bytes 524320 | tf_op jit(solution)/shard_map/ppermute | solution.py:25
  198.5 1.6 collective-permute-start.34
  200.1 1.0 add_convert_fusion.3
  201.1 7.2 %collective-permute-done.39 = bf16[512,512]{1,0:T(8,128)(2,1)S(1)} collective-permute-done((bf16[512,512]{1,0:T(8,128)(2,1)S(1)}, bf16[512,512]{1,0:T(8,128)(2,1)S(1)}, u32[]{:S(2)}, u32[]{:S(2)}) %collective-permute-start.39) | collective-permute-done | bytes 524320 | tf_op jit(solution)/shard_map/ppermute | solution.py:25
  208.3 1.7 collective-permute-done.34
  210.6 2.1 collective-permute-start.40
  212.7 7.5 %collective-permute-done.35 = bf16[2,128,512]{2,1,0:T(8,128)(2,1)S(1)} collective-permute-done((bf16[2,128,512]{2,1,0:T(8,128)(2,1)S(1)}, bf16[2,128,512]{2,1,0:T(8,128)(2,1)S(1)}, u32[]{:S(2)}, u32[]{:S(2)}) %collective-permute-start.35) | collective-permute-done | bytes 262176 | tf_op jit(solution)/shard_map/ppermute | solution.py:25
  220.3 2.7 %collective-permute-done.40 = bf16[2,128,512]{2,1,0:T(8,128)(2,1)S(1)} collective-permute-done((bf16[2,128,512]{2,1,0:T(8,128)(2,1)S(1)}, bf16[2,128,512]{2,1,0:T(8,128)(2,1)S(1)}, u32[]{:S(2)}, u32[]{:S(2)}) %collective-permute-start.40) | collective-permute-done | bytes 262176 | tf_op jit(solution)/shard_map/ppermute | solution.py:25
  223.4 4.2 %collective-permute-done.36 = bf16[128,512]{1,0:T(8,128)(2,1)S(1)} collective-permute-done((bf16[128,512]{1,0:T(8,128)(2,1)S(1)}, bf16[128,512]{1,0:T(8,128)(2,1)S(1)}, u32[]{:S(2)}, u32[]{:S(2)}) %collective-permute-start.36) | collective-permute-done | bytes 131104 | tf_op jit(solution)/shard_map/ppermute | solution.py:25
  227.6 2.8 %collective-permute-done.41 = bf16[128,512]{1,0:T(8,128)(2,1)S(1)} collective-permute-done((bf16[128,512]{1,0:T(8,128)(2,1)S(1)}, bf16[128,512]{1,0:T(8,128)(2,1)S(1)}, u32[]{:S(2)}, u32[]{:S(2)}) %collective-permute-start.41) | collective-permute-done | bytes 131104 | tf_op jit(solution)/shard_map/ppermute | solution.py:25
  (124 shorter events, 17.6 us)
Async XLA Ops:
  0.0 151.5 %copy-start = (bf16[1,704,2048]{2,1,0:T(8,128)(2,1)S(1)}, bf16[1,704,2048]{2,1,0:T(8,128)(2,1)}, u32[]{:S(2)}) copy-start(bf16[1,704,2048]{2,1,0:T(8,128)(2,1)} %param.19) | copy-start | bytes 8650756
  0.0 6.2 %copy-start.14 = (s32[1,4]{1,0:T(1,128)S(1)}, s32[1,4]{1,0:T(1,128)}, u32[]{:S(2)}) copy-start(s32[1,4]{1,0:T(1,128)} %param.11) | copy-start | bytes 52
  0.0 54.5 %collective-permute-start.1 = (bf16[1152,1024]{1,0:T(8,128)(2,1)}, bf16[1152,1024]{1,0:T(8,128)(2,1)}, u32[]{:S(2)}, u32[]{:S(2)}) collective-permute-start(bf16[1152,1024]{1,0:T(8,128)(2,1)} %param.14), channel_id=1, source_target_pairs={{0,8},{4,12},{8,0},{12,4},{1,9},{5,13},{9,1},{13,5},{2,10},{6,14},... | collective-permute-start | bytes 7077896 | tf_op jit(solution)/shard_map/ppermute | solution.py:25
  21.2 4.5 %copy-start.13 = (bf16[576,1152]{1,0:T(8,128)(2,1)S(1)}, bf16[576,1152]{1,0:T(8,128)(2,1)}, u32[]{:S(2)}) copy-start(bf16[576,1152]{1,0:T(8,128)(2,1)} %param.13) | copy-start | bytes 3981316
  28.0 27.7 %collective-permute-start = (bf16[512,1152]{1,0:T(8,128)(2,1)}, bf16[512,1152]{1,0:T(8,128)(2,1)}, u32[]{:S(2)}, u32[]{:S(2)}) collective-permute-start(bf16[512,1152]{1,0:T(8,128)(2,1)} %convolution_convert_fusion.1), channel_id=1, source_target_pairs={{0,16},{16,0},{1,17},{17,1},{2,18},{18,2},{3,19},{19,3},{4,20},{20... | collective-permute-start | bytes 3538952 | tf_op jit(solution)/shard_map/ppermute | solution.py:25
  29.5 36.9 %collective-permute-start.2 = (bf16[1152,1024]{1,0:T(8,128)(2,1)}, bf16[1152,1024]{1,0:T(8,128)(2,1)}, u32[]{:S(2)}, u32[]{:S(2)}) collective-permute-start(bf16[1152,1024]{1,0:T(8,128)(2,1)} %param.14), channel_id=1, source_target_pairs={{0,4},{4,0},{8,12},{12,8},{1,5},{5,1},{9,13},{13,9},{2,6},{6,2},{1... | collective-permute-start | bytes 7077896 | tf_op jit(solution)/shard_map/ppermute | solution.py:25
  54.5 14.1 %collective-permute-start.3 = (bf16[1152,1024]{1,0:T(8,128)(2,1)}, bf16[1152,1024]{1,0:T(8,128)(2,1)}, u32[]{:S(2)}, u32[]{:S(2)}) collective-permute-start(bf16[1152,1024]{1,0:T(8,128)(2,1)} %collective-permute-done.1), channel_id=1, source_target_pairs={{0,4},{4,0},{8,12},{12,8},{1,5},{5,1},{9,13},{13,9},{2,6},{6,2},{1... | collective-permute-start | bytes 7077896 | tf_op jit(solution)/shard_map/ppermute | solution.py:25
  61.8 2.4 %copy-start.1 = (bf16[128,4608]{1,0:T(8,128)(2,1)S(1)}, bf16[128,4608]{1,0:T(8,128)(2,1)}, u32[]{:S(2)}) copy-start(bf16[128,4608]{1,0:T(8,128)(2,1)} %convert_element_type.230) | copy-start | bytes 3538948
  71.0 19.6 %copy-start.11 = (f32[128,6]{0,1:T(8,128)S(1)}, f32[128,6]{0,1:T(8,128)}, u32[]{:S(2)}) copy-start(f32[128,6]{0,1:T(8,128)} %param.16) | copy-start | bytes 9220
  71.0 19.6 %copy-start.12 = (s32[128,6]{0,1:T(8,128)S(1)}, s32[128,6]{0,1:T(8,128)}, u32[]{:S(2)}) copy-start(s32[128,6]{0,1:T(8,128)} %param.15) | copy-start | bytes 9220
  71.0 3.6 %collective-permute-start.4 = (f32[128]{0:T(128)S(1)}, f32[128]{0:T(128)S(1)}, u32[]{:S(2)}, u32[]{:S(2)}) collective-permute-start(f32[128]{0:T(128)S(1)} %get-tuple-element.48), channel_id=1, source_target_pairs={{0,16},{16,0},{1,17},{17,1},{2,18},{18,2},{3,19},{19,3},{4,20},{20... | collective-permute-start | bytes 1544 | tf_op jit(solution)/shard_map/ppermute | solution.py:25
  74.8 11.6 %copy-start.6 = (bf16[1,128,512]{2,1,0:T(8,128)(2,1)}, bf16[1,128,512]{2,1,0:T(8,128)(2,1)S(1)}, u32[]{:S(2)}) copy-start(bf16[1,128,512]{2,1,0:T(8,128)(2,1)S(1)} %get-tuple-element.42) | copy-start | bytes 393220
  74.8 11.6 %collective-permute-start.7 = (bf16[128,512]{1,0:T(8,128)(2,1)S(1)}, bf16[128,512]{1,0:T(8,128)(2,1)S(1)}, u32[]{:S(2)}, u32[]{:S(2)}) collective-permute-start(bf16[128,512]{1,0:T(8,128)(2,1)S(1)} %get-tuple-element.44), channel_id=1, source_target_pairs={{0,2},{1,3},{2,0},{3,1},{4,6},{5,7},{6,4},{7,5},{8,10},{9,11},{10,... | collective-permute-start | bytes 393224 | tf_op jit(solution)/shard_map/ppermute | solution.py:25
  77.4 10.5 %collective-permute-start.5 = (bf16[128,512]{1,0:T(8,128)(2,1)S(1)}, bf16[128,512]{1,0:T(8,128)(2,1)S(1)}, u32[]{:S(2)}, u32[]{:S(2)}) collective-permute-start(bf16[128,512]{1,0:T(8,128)(2,1)S(1)} %get-tuple-element.45), channel_id=1, source_target_pairs={{0,2},{1,3},{2,0},{3,1},{4,6},{5,7},{6,4},{7,5},{8,10},{9,11},{10,... | collective-permute-start | bytes 393224 | tf_op jit(solution)/shard_map/ppermute | solution.py:25
  86.4 2.9 %copy-start.8 = (bf16[128,512]{1,0:T(8,128)(2,1)}, bf16[128,512]{1,0:T(8,128)(2,1)S(1)}, u32[]{:S(2)}) copy-start(bf16[128,512]{1,0:T(8,128)(2,1)S(1)} %collective-permute-done.7) | copy-start | bytes 393220
  87.2 15.3 %collective-permute-start.8 = (bf16[2,128,512]{2,1,0:T(8,128)(2,1)}, bf16[2,128,512]{2,1,0:T(8,128)(2,1)}, u32[]{:S(2)}, u32[]{:S(2)}) collective-permute-start(bf16[2,128,512]{2,1,0:T(8,128)(2,1)} %pad_maximum_fusion.10), channel_id=1, source_target_pairs={{0,1},{1,0},{2,3},{3,2},{4,5},{5,4},{6,7},{7,6},{8,9},{9,8},{10,11... | collective-permute-start | bytes 786440 | tf_op jit(solution)/shard_map/ppermute | solution.py:25
  87.9 0.7 copy-start.7
  89.3 16.6 %collective-permute-start.6 = (bf16[2,128,512]{2,1,0:T(8,128)(2,1)}, bf16[2,128,512]{2,1,0:T(8,128)(2,1)}, u32[]{:S(2)}, u32[]{:S(2)}) collective-permute-start(bf16[2,128,512]{2,1,0:T(8,128)(2,1)} %pad_maximum_fusion.9), channel_id=1, source_target_pairs={{0,1},{1,0},{2,3},{3,2},{4,5},{5,4},{6,7},{7,6},{8,9},{9,8},{10,11... | collective-permute-start | bytes 786440 | tf_op jit(solution)/shard_map/ppermute | solution.py:25
  90.6 7.7 %collective-permute-start.11 = (f32[128,16]{0,1:T(8,128)S(1)}, f32[128,16]{0,1:T(8,128)S(1)}, u32[]{:S(2)}, u32[]{:S(2)}) collective-permute-start(f32[128,16]{0,1:T(8,128)S(1)} %select_reduce_fusion), channel_id=1, source_target_pairs={{0,2},{1,3},{2,0},{3,1},{4,6},{5,7},{6,4},{7,5},{8,10},{9,11},{10,... | collective-permute-start | bytes 24584 | tf_op jit(solution)/shard_map/ppermute | solution.py:25
  98.3 9.9 %collective-permute-start.12 = (f32[2,128,16]{1,2,0:T(8,128)S(1)}, f32[2,128,16]{1,2,0:T(8,128)S(1)}, u32[]{:S(2)}, u32[]{:S(2)}) collective-permute-start(f32[2,128,16]{1,2,0:T(8,128)S(1)} %pad_maximum_fusion.12), channel_id=1, source_target_pairs={{0,1},{1,0},{2,3},{3,2},{4,5},{5,4},{6,7},{7,6},{8,9},{9,8},{10,11... | collective-permute-start | bytes 49160 | tf_op jit(solution)/shard_map/ppermute | solution.py:25
  104.3 15.2 %collective-permute-start.10 = (bf16[512,512]{1,0:T(8,128)(2,1)}, bf16[512,512]{1,0:T(8,128)(2,1)}, u32[]{:S(2)}, u32[]{:S(2)}) collective-permute-start(bf16[512,512]{1,0:T(8,128)(2,1)} %bitcast.13), channel_id=1, source_target_pairs={{0,16},{16,0},{1,17},{17,1},{2,18},{18,2},{3,19},{19,3},{4,20},{20... | collective-permute-start | bytes 1572872 | tf_op jit(solution)/shard_map/ppermute | solution.py:25
  107.7 20.8 %collective-permute-start.9 = (bf16[512,512]{1,0:T(8,128)(2,1)}, bf16[512,512]{1,0:T(8,128)(2,1)}, u32[]{:S(2)}, u32[]{:S(2)}) collective-permute-start(bf16[512,512]{1,0:T(8,128)(2,1)} %bitcast.10), channel_id=1, source_target_pairs={{0,16},{16,0},{1,17},{17,1},{2,18},{18,2},{3,19},{19,3},{4,20},{20... | collective-permute-start | bytes 1572872 | tf_op jit(solution)/shard_map/ppermute | solution.py:25
  108.2 0.6 copy-start.9
  109.5 8.2 %copy-start.10 = (f32[2,128,16]{1,2,0:T(8,128)S(1)}, f32[2,128,16]{1,2,0:T(8,128)}, u32[]{:S(2)}) copy-start(f32[2,128,16]{1,2,0:T(8,128)} %copy-done.9) | copy-start | bytes 49156
  109.5 6.8 %collective-permute-start.25 = (f32[4,128,16]{1,2,0:T(8,128)}, f32[4,128,16]{1,2,0:T(8,128)S(1)}, u32[]{:S(2)}, u32[]{:S(2)}) collective-permute-start(f32[4,128,16]{1,2,0:T(8,128)} %pad_maximum_fusion.11), channel_id=1, source_target_pairs={{0,8},{4,12},{8,0},{12,4},{1,9},{5,13},{9,1},{13,5},{2,10},{6,14},... | collective-permute-start | bytes 98312 | tf_op jit(solution)/shard_map/ppermute | solution.py:25
  116.2 1.4 collective-permute-start.17
  116.2 1.4 collective-permute-start.30
  117.8 28.4 %collective-permute-start.14 = (bf16[512,512]{1,0:T(8,128)(2,1)}, bf16[512,512]{1,0:T(8,128)(2,1)S(1)}, u32[]{:S(2)}, u32[]{:S(2)}) collective-permute-start(bf16[512,512]{1,0:T(8,128)(2,1)} %bitcast.13), channel_id=1, source_target_pairs={{0,4},{4,0},{8,12},{12,8},{1,5},{5,1},{9,13},{13,9},{2,6},{6,2},{1... | collective-permute-start | bytes 1572872 | tf_op jit(solution)/shard_map/ppermute | solution.py:25
  118.1 18.1 %collective-permute-start.13 = (bf16[512,512]{1,0:T(8,128)(2,1)}, bf16[512,512]{1,0:T(8,128)(2,1)S(1)}, u32[]{:S(2)}, u32[]{:S(2)}) collective-permute-start(bf16[512,512]{1,0:T(8,128)(2,1)} %bitcast.10), channel_id=1, source_target_pairs={{0,4},{4,0},{8,12},{12,8},{1,5},{5,1},{9,13},{13,9},{2,6},{6,2},{1... | collective-permute-start | bytes 1572872 | tf_op jit(solution)/shard_map/ppermute | solution.py:25
  118.3 18.5 %collective-permute-start.22 = (bf16[512,512]{1,0:T(8,128)(2,1)}, bf16[512,512]{1,0:T(8,128)(2,1)S(1)}, u32[]{:S(2)}, u32[]{:S(2)}) collective-permute-start(bf16[512,512]{1,0:T(8,128)(2,1)} %bitcast.13), channel_id=1, source_target_pairs={{0,8},{4,12},{8,0},{12,4},{1,9},{5,13},{9,1},{13,5},{2,10},{6,14},... | collective-permute-start | bytes 1572872 | tf_op jit(solution)/shard_map/ppermute | solution.py:25
  119.5 25.0 %collective-permute-start.21 = (bf16[512,512]{1,0:T(8,128)(2,1)}, bf16[512,512]{1,0:T(8,128)(2,1)S(1)}, u32[]{:S(2)}, u32[]{:S(2)}) collective-permute-start(bf16[512,512]{1,0:T(8,128)(2,1)} %bitcast.10), channel_id=1, source_target_pairs={{0,8},{4,12},{8,0},{12,4},{1,9},{5,13},{9,1},{13,5},{2,10},{6,14},... | collective-permute-start | bytes 1572872 | tf_op jit(solution)/shard_map/ppermute | solution.py:25
  128.5 17.8 %collective-permute-start.15 = (bf16[512,512]{1,0:T(8,128)(2,1)}, bf16[512,512]{1,0:T(8,128)(2,1)S(1)}, u32[]{:S(2)}, u32[]{:S(2)}) collective-permute-start(bf16[512,512]{1,0:T(8,128)(2,1)} %collective-permute-done.9), channel_id=1, source_target_pairs={{0,4},{4,0},{8,12},{12,8},{1,5},{5,1},{9,13},{13,9},{2,6},{6,2},{1... | collective-permute-start | bytes 1572872 | tf_op jit(solution)/shard_map/ppermute | solution.py:25
  128.5 4.3 %copy-start.2 = (bf16[1024,704]{0,1:T(8,128)(2,1)S(1)}, bf16[1024,704]{0,1:T(8,128)(2,1)}, u32[]{:S(2)}) copy-start(bf16[1024,704]{0,1:T(8,128)(2,1)} %get-tuple-element.28) | copy-start | bytes 4325380
  128.5 4.3 %copy-start.3 = (bf16[1024,704]{0,1:T(8,128)(2,1)S(1)}, bf16[1024,704]{0,1:T(8,128)(2,1)}, u32[]{:S(2)}) copy-start(bf16[1024,704]{0,1:T(8,128)(2,1)} %get-tuple-element.30) | copy-start | bytes 4325380
  136.2 10.8 %collective-permute-start.16 = (bf16[512,512]{1,0:T(8,128)(2,1)}, bf16[512,512]{1,0:T(8,128)(2,1)S(1)}, u32[]{:S(2)}, u32[]{:S(2)}) collective-permute-start(bf16[512,512]{1,0:T(8,128)(2,1)} %collective-permute-done.10), channel_id=1, source_target_pairs={{0,4},{4,0},{8,12},{12,8},{1,5},{5,1},{9,13},{13,9},{2,6},{6,2},{1... | collective-permute-start | bytes 1572872 | tf_op jit(solution)/shard_map/ppermute | solution.py:25
  136.9 18.3 %collective-permute-start.23 = (bf16[512,512]{1,0:T(8,128)(2,1)}, bf16[512,512]{1,0:T(8,128)(2,1)S(1)}, u32[]{:S(2)}, u32[]{:S(2)}) collective-permute-start(bf16[512,512]{1,0:T(8,128)(2,1)} %collective-permute-done.9), channel_id=1, source_target_pairs={{0,8},{4,12},{8,0},{12,4},{1,9},{5,13},{9,1},{13,5},{2,10},{6,14},... | collective-permute-start | bytes 1572872 | tf_op jit(solution)/shard_map/ppermute | solution.py:25
  144.5 12.7 %collective-permute-start.24 = (bf16[512,512]{1,0:T(8,128)(2,1)S(1)}, bf16[512,512]{1,0:T(8,128)(2,1)S(1)}, u32[]{:S(2)}, u32[]{:S(2)}) collective-permute-start(bf16[512,512]{1,0:T(8,128)(2,1)S(1)} %collective-permute-done.22), channel_id=1, source_target_pairs={{0,16},{16,0},{1,17},{17,1},{2,18},{18,2},{3,19},{19,3},{4,20},{20... | collective-permute-start | bytes 1572872 | tf_op jit(solution)/shard_map/ppermute | solution.py:25
  146.1 1.4 copy-start.4
  146.1 1.8 copy-start.5
  146.2 11.3 %collective-permute-start.27 = (bf16[512,512]{1,0:T(8,128)(2,1)S(1)}, bf16[512,512]{1,0:T(8,128)(2,1)S(1)}, u32[]{:S(2)}, u32[]{:S(2)}) collective-permute-start(bf16[512,512]{1,0:T(8,128)(2,1)S(1)} %collective-permute-done.22), channel_id=1, source_target_pairs={{0,4},{4,0},{8,12},{12,8},{1,5},{5,1},{9,13},{13,9},{2,6},{6,2},{1... | collective-permute-start | bytes 1572872 | tf_op jit(solution)/shard_map/ppermute | solution.py:25
  146.3 11.0 %collective-permute-start.26 = (bf16[512,512]{1,0:T(8,128)(2,1)S(1)}, bf16[512,512]{1,0:T(8,128)(2,1)S(1)}, u32[]{:S(2)}, u32[]{:S(2)}) collective-permute-start(bf16[512,512]{1,0:T(8,128)(2,1)S(1)} %collective-permute-done.21), channel_id=1, source_target_pairs={{0,4},{4,0},{8,12},{12,8},{1,5},{5,1},{9,13},{13,9},{2,6},{6,2},{1... | collective-permute-start | bytes 1572872 | tf_op jit(solution)/shard_map/ppermute | solution.py:25
  152.5 18.5 %collective-permute-start.19 = (bf16[512,1024]{1,0:T(8,128)(2,1)S(1)}, bf16[512,1024]{1,0:T(8,128)(2,1)S(1)}, u32[]{:S(2)}, u32[]{:S(2)}) collective-permute-start(bf16[512,1024]{1,0:T(8,128)(2,1)S(1)} %multiply_convert_fusion.4), channel_id=1, source_target_pairs={{0,4},{4,0},{8,12},{12,8},{1,5},{5,1},{9,13},{13,9},{2,6},{6,2},{1... | collective-permute-start | bytes 3145736 | tf_op jit(solution)/shard_map/ppermute | solution.py:25
  155.1 4.4 %collective-permute-start.28 = (bf16[512,512]{1,0:T(8,128)(2,1)S(1)}, bf16[512,512]{1,0:T(8,128)(2,1)S(1)}, u32[]{:S(2)}, u32[]{:S(2)}) collective-permute-start(bf16[512,512]{1,0:T(8,128)(2,1)S(1)} %collective-permute-done.23), channel_id=1, source_target_pairs={{0,4},{4,0},{8,12},{12,8},{1,5},{5,1},{9,13},{13,9},{2,6},{6,2},{1... | collective-permute-start | bytes 1572872 | tf_op jit(solution)/shard_map/ppermute | solution.py:25
  157.2 2.4 %collective-permute-start.29 = (bf16[512,512]{1,0:T(8,128)(2,1)S(1)}, bf16[512,512]{1,0:T(8,128)(2,1)S(1)}, u32[]{:S(2)}, u32[]{:S(2)}) collective-permute-start(bf16[512,512]{1,0:T(8,128)(2,1)S(1)} %collective-permute-done.24), channel_id=1, source_target_pairs={{0,4},{4,0},{8,12},{12,8},{1,5},{5,1},{9,13},{13,9},{2,6},{6,2},{1... | collective-permute-start | bytes 1572872 | tf_op jit(solution)/shard_map/ppermute | solution.py:25
  164.3 5.1 %collective-permute-start.32 = (bf16[512,1024]{1,0:T(8,128)(2,1)S(1)}, bf16[512,1024]{1,0:T(8,128)(2,1)S(1)}, u32[]{:S(2)}, u32[]{:S(2)}) collective-permute-start(bf16[512,1024]{1,0:T(8,128)(2,1)S(1)} %multiply_convert_fusion), channel_id=1, source_target_pairs={{0,4},{4,0},{8,12},{12,8},{1,5},{5,1},{9,13},{13,9},{2,6},{6,2},{1... | collective-permute-start | bytes 3145736 | tf_op jit(solution)/shard_map/ppermute | solution.py:25
  167.7 6.5 %collective-permute-start.31 = (bf16[512,1024]{1,0:T(8,128)(2,1)S(1)}, bf16[512,1024]{1,0:T(8,128)(2,1)S(1)}, u32[]{:S(2)}, u32[]{:S(2)}) collective-permute-start(bf16[512,1024]{1,0:T(8,128)(2,1)S(1)} %multiply_convert_fusion.2), channel_id=1, source_target_pairs={{0,4},{4,0},{8,12},{12,8},{1,5},{5,1},{9,13},{13,9},{2,6},{6,2},{1... | collective-permute-start | bytes 3145736 | tf_op jit(solution)/shard_map/ppermute | solution.py:25
  168.8 31.2 %collective-permute-start.18 = (bf16[512,1024]{1,0:T(8,128)(2,1)S(1)}, bf16[512,1024]{1,0:T(8,128)(2,1)S(1)}, u32[]{:S(2)}, u32[]{:S(2)}) collective-permute-start(bf16[512,1024]{1,0:T(8,128)(2,1)S(1)} %multiply_convert_fusion.6), channel_id=1, source_target_pairs={{0,4},{4,0},{8,12},{12,8},{1,5},{5,1},{9,13},{13,9},{2,6},{6,2},{1... | collective-permute-start | bytes 3145736 | tf_op jit(solution)/shard_map/ppermute | solution.py:25
  170.5 14.9 %collective-permute-start.38 = (bf16[512,512]{1,0:T(8,128)(2,1)S(1)}, bf16[512,512]{1,0:T(8,128)(2,1)S(1)}, u32[]{:S(2)}, u32[]{:S(2)}) collective-permute-start(bf16[512,512]{1,0:T(8,128)(2,1)S(1)} %get-tuple-element.37), channel_id=1, source_target_pairs={{0,8},{4,12},{8,0},{12,4},{1,9},{5,13},{9,1},{13,5},{2,10},{6,14},... | collective-permute-start | bytes 1572872 | tf_op jit(solution)/shard_map/ppermute | solution.py:25
  172.2 28.9 %collective-permute-start.20 = (bf16[512,512]{1,0:T(8,128)(2,1)S(1)}, bf16[512,512]{1,0:T(8,128)(2,1)S(1)}, u32[]{:S(2)}, u32[]{:S(2)}) collective-permute-start(bf16[512,512]{1,0:T(8,128)(2,1)S(1)} %slice.100), channel_id=1, source_target_pairs={{0,16},{16,0},{1,17},{17,1},{2,18},{18,2},{3,19},{19,3},{4,20},{20... | collective-permute-start | bytes 1572872 | tf_op jit(solution)/shard_map/ppermute | solution.py:25
  173.7 24.6 %collective-permute-start.33 = (bf16[512,512]{1,0:T(8,128)(2,1)S(1)}, bf16[512,512]{1,0:T(8,128)(2,1)S(1)}, u32[]{:S(2)}, u32[]{:S(2)}) collective-permute-start(bf16[512,512]{1,0:T(8,128)(2,1)S(1)} %get-tuple-element.36), channel_id=1, source_target_pairs={{0,16},{16,0},{1,17},{17,1},{2,18},{18,2},{3,19},{19,3},{4,20},{20... | collective-permute-start | bytes 1572872 | tf_op jit(solution)/shard_map/ppermute | solution.py:25
  175.3 25.8 %collective-permute-start.37 = (bf16[512,512]{1,0:T(8,128)(2,1)S(1)}, bf16[512,512]{1,0:T(8,128)(2,1)S(1)}, u32[]{:S(2)}, u32[]{:S(2)}) collective-permute-start(bf16[512,512]{1,0:T(8,128)(2,1)S(1)} %slice.108), channel_id=1, source_target_pairs={{0,8},{4,12},{8,0},{12,4},{1,9},{5,13},{9,1},{13,5},{2,10},{6,14},... | collective-permute-start | bytes 1572872 | tf_op jit(solution)/shard_map/ppermute | solution.py:25
  185.5 22.7 %collective-permute-start.39 = (bf16[512,512]{1,0:T(8,128)(2,1)S(1)}, bf16[512,512]{1,0:T(8,128)(2,1)S(1)}, u32[]{:S(2)}, u32[]{:S(2)}) collective-permute-start(bf16[512,512]{1,0:T(8,128)(2,1)S(1)} %add_convert_fusion.5), channel_id=1, source_target_pairs={{0,16},{16,0},{1,17},{17,1},{2,18},{18,2},{3,19},{19,3},{4,20},{20... | collective-permute-start | bytes 1572872 | tf_op jit(solution)/shard_map/ppermute | solution.py:25
  198.5 11.5 %collective-permute-start.34 = (bf16[512,512]{1,0:T(8,128)(2,1)S(1)}, bf16[512,512]{1,0:T(8,128)(2,1)S(1)}, u32[]{:S(2)}, u32[]{:S(2)}) collective-permute-start(bf16[512,512]{1,0:T(8,128)(2,1)S(1)} %add_convert_fusion.8), channel_id=1, source_target_pairs={{0,8},{4,12},{8,0},{12,4},{1,9},{5,13},{9,1},{13,5},{2,10},{6,14},... | collective-permute-start | bytes 1572872 | tf_op jit(solution)/shard_map/ppermute | solution.py:25
  210.5 9.7 %collective-permute-start.35 = (bf16[2,128,512]{2,1,0:T(8,128)(2,1)S(1)}, bf16[2,128,512]{2,1,0:T(8,128)(2,1)S(1)}, u32[]{:S(2)}, u32[]{:S(2)}) collective-permute-start(bf16[2,128,512]{2,1,0:T(8,128)(2,1)S(1)} %bitcast.134), channel_id=1, source_target_pairs={{0,1},{1,0},{2,3},{3,2},{4,5},{5,4},{6,7},{7,6},{8,9},{9,8},{10,11... | collective-permute-start | bytes 786440 | tf_op jit(solution)/shard_map/ppermute | solution.py:25
  210.6 12.4 %collective-permute-start.40 = (bf16[2,128,512]{2,1,0:T(8,128)(2,1)S(1)}, bf16[2,128,512]{2,1,0:T(8,128)(2,1)S(1)}, u32[]{:S(2)}, u32[]{:S(2)}) collective-permute-start(bf16[2,128,512]{2,1,0:T(8,128)(2,1)S(1)} %bitcast.133), channel_id=1, source_target_pairs={{0,1},{1,0},{2,3},{3,2},{4,5},{5,4},{6,7},{7,6},{8,9},{9,8},{10,11... | collective-permute-start | bytes 786440 | tf_op jit(solution)/shard_map/ppermute | solution.py:25
  220.2 7.3 %collective-permute-start.36 = (bf16[128,512]{1,0:T(8,128)(2,1)S(1)}, bf16[128,512]{1,0:T(8,128)(2,1)S(1)}, u32[]{:S(2)}, u32[]{:S(2)}) collective-permute-start(bf16[128,512]{1,0:T(8,128)(2,1)S(1)} %slice_bitcast_fusion.16), channel_id=1, source_target_pairs={{0,2},{1,3},{2,0},{3,1},{4,6},{5,7},{6,4},{7,5},{8,10},{9,11},{10,... | collective-permute-start | bytes 393224 | tf_op jit(solution)/shard_map/ppermute | solution.py:25
  223.1 7.3 %collective-permute-start.41 = (bf16[128,512]{1,0:T(8,128)(2,1)S(1)}, bf16[128,512]{1,0:T(8,128)(2,1)S(1)}, u32[]{:S(2)}, u32[]{:S(2)}) collective-permute-start(bf16[128,512]{1,0:T(8,128)(2,1)S(1)} %slice_bitcast_fusion.14), channel_id=1, source_target_pairs={{0,2},{1,3},{2,0},{3,1},{4,6},{5,7},{6,4},{7,5},{8,10},{9,11},{10,... | collective-permute-start | bytes 393224 | tf_op jit(solution)/shard_map/ppermute | solution.py:25
